TPU v7x, 32 devices: a whole 2x2x4 slice. The times are simulated.
32 devices in a mesh: gx: 4 (over y, x), gy: 2 (over core), gz: 4 (over z).
Axes of the slice: x: 2, y: 2, z: 4, core: 2. Of those that a mesh axis runs over, the one named last changes fastest.
Arguments:
- basis: bfloat16 [8, 3, 16, 512, 128], P('gx', None, 'gy', 'gz'), may hold values from -4.8 to 4.8
- modal_now: bfloat16 [128, 8], replicated, may hold values from -0.5 to 0.5
- modal_prev: bfloat16 [128, 8], replicated, may hold values from -0.5 to 0.5
- material_ids: int32 [8, 16, 512], P('gx', 'gy', 'gz'), may hold values from 0 to 3
- moduli: float32 [3, 4], replicated, may hold values from 0.4 to 1.6
- drive_mask: int32 [8, 8, 16, 512], P(None, 'gx', 'gy', 'gz'), may hold values 0 or 1
- drive: float32 [3, 8], replicated, may hold values from -8 to 8
Outputs:
- displacement: float32 [3, 8, 8, 16, 512], P(None, None, 'gx', 'gy', 'gz')
- modes: float32 [3, 8, 8, 16, 512], P(None, None, 'gx', 'gy', 'gz')
- coefficients: float32 [4, 2, 128, 8], replicated
- rfactor: float32 [4, 8, 8], replicated
All inputs are finite; a program needn't handle non-finite values. No bound on the sum of `drive_mask` on one device may be relied on, other than what follows from the above.
Results may differ from a plain program's by a relative error of at most 0.0008.
The roundings to bfloat16 on the way count: a program that leaves them out, or rounds other values in their place, can miss the bound.
Values sent between devices are 32-bit elements; how exact they have to be, the bound alone decides.
A program may use at most 128 MiB of HBM per device.

v0:
```python
import jax
import jax.numpy as jnp
from jax import lax
from jax.sharding import PartitionSpec as P

STEPS = 4


step_squared = 0.1
ramp_steps = 4.0


def padded_2(block, sides, width):
    for axis, dim in sides:
        count = lax.axis_size(axis)
        forward = [(i, i + 1) for i in range(count - 1)]
        backward = [(target, source) for source, target in forward]
        low = lax.ppermute(
            lax.slice_in_dim(block, block.shape[dim] - width, None, axis=dim), axis, forward
        )
        high = lax.ppermute(lax.slice_in_dim(block, 0, width, axis=dim), axis, backward)
        block = jnp.concatenate([low, block, high], axis=dim)
    return block


def interior(array, direction_axis, offset):
    base_axis = array.ndim - 3
    result = array
    for axis_index in range(3):
        extent = array.shape[base_axis + axis_index]
        begin = offset if axis_index == direction_axis else 1
        result = lax.slice_in_dim(result, begin, extent - 2 + begin, axis=base_axis + axis_index)
    return result


def stiffness(field, material_props):
    component_rows = []
    for component in range(3):
        center = interior(field[component], 0, 1)
        accumulated = jnp.zeros_like(center)
        for direction_axis in range(3):
            modulus = material_props[0] if component == direction_axis else material_props[1]
            center_modulus = interior(modulus, 0, 1)
            for offset in (0, 2):
                coupling = 0.5 * (center_modulus + interior(modulus, direction_axis, offset))
                accumulated = accumulated + coupling * (
                    center - interior(field[component], direction_axis, offset)
                )
        component_rows.append(accumulated)
    return jnp.stack(component_rows)


def lookup(material_ids, moduli):
    levels = jnp.arange(moduli.shape[1], dtype=jnp.int32)
    onehot = (material_ids[None] == levels[:, None, None, None]).astype(jnp.float32)
    return jnp.einsum("mxyz,pm->pxyz", onehot, moduli, precision=lax.Precision.HIGHEST)


def expand(basis, coefficient):
    return jnp.einsum("xcyzk,kj->cjxyz", basis, coefficient, preferred_element_type=jnp.float32)


def project(basis, field):
    return jnp.einsum("xcyzk,cjxyz->kj", basis, field, preferred_element_type=jnp.float32)


def apply_inverse(block, lower_factor):
    identity_block = jnp.eye(lower_factor.shape[0], dtype=jnp.float32)
    lower_inverse = jax.scipy.linalg.solve_triangular(lower_factor, identity_block, lower=True)
    return jnp.einsum("cixyz,ji->cjxyz", block, lower_inverse, precision=lax.Precision.HIGHEST)


def local_gram(block):
    return jnp.einsum("cixyz,cjxyz->ij", block, block, precision=lax.Precision.HIGHEST)


def orthonormalize(following, basis, dof_weight):
    highest = lax.Precision.HIGHEST
    snapshot = following.astype(jnp.bfloat16)
    partial_coef = project(basis, snapshot) * dof_weight
    first_coef = lax.psum(partial_coef, ("gx", "gy", "gz"))
    first_resid = snapshot.astype(jnp.float32) - expand(basis, first_coef.astype(jnp.bfloat16))
    first_gram = lax.psum(local_gram(first_resid) * dof_weight, ("gx", "gy", "gz"))
    first_lower = jnp.linalg.cholesky(first_gram)
    first_q = apply_inverse(first_resid, first_lower)
    second_coef = lax.psum(
        project(basis, first_q.astype(jnp.bfloat16)) * dof_weight, ("gx", "gy", "gz")
    )
    second_resid = first_q - expand(basis, second_coef.astype(jnp.bfloat16))
    second_gram = lax.psum(local_gram(second_resid) * dof_weight, ("gx", "gy", "gz"))
    second_lower = jnp.linalg.cholesky(second_gram)
    modes = apply_inverse(second_resid, second_lower)
    factor = jnp.dot(first_lower, second_lower, precision=highest).T
    return (jnp.stack([first_coef, second_coef]), factor, modes)


def shards(basis, modal_now, modal_prev, material_ids, moduli, drive_mask, drive):
    devices_total = lax.axis_size("gx") * lax.axis_size("gy") * lax.axis_size("gz")
    dof_weight = 1.0 / (3.0 * basis.shape[0] * basis.shape[2] * basis.shape[3] * devices_total)
    current = expand(basis, modal_now)
    earlier = expand(basis, modal_prev)
    material_props = lookup(material_ids, moduli)
    port_mask = drive_mask.astype(jnp.float32)
    static = jnp.concatenate([material_props, port_mask], axis=0)
    wide_static = padded_2(static, (("gx", 1), ("gy", 2), ("gz", 3)), 2)
    props_wide = wide_static[:3]
    props_near = props_wide[:, 1:-1, 1:-1, 1:-1]
    inverse_mass = material_props[2]
    drive_field = drive[:, :, None, None, None]
    coefficient_list = []
    factor_list = []
    modes = current
    for step in range(STEPS):
        padded = padded_2(current, (("gx", 2), ("gy", 3), ("gz", 4)), 1)
        ramp_level = min(1.0, (step + 1) / ramp_steps)
        load_field = drive_field * port_mask[None] * ramp_level
        following = (
            2.0 * current
            - earlier
            + step_squared * inverse_mass * (load_field - stiffness(padded, props_near))
        )
        earlier = current
        current = following
        coefs, factor, modes = orthonormalize(following, basis, dof_weight)
        coefficient_list.append(coefs)
        factor_list.append(factor)
    return (current, modes, jnp.stack(coefficient_list), jnp.stack(factor_list))


def solution(mesh):
    in_specs = (
        P("gx", None, "gy", "gz", None),
        P(),
        P(),
        P("gx", "gy", "gz"),
        P(),
        P(None, "gx", "gy", "gz"),
        P(),
    )
    out_specs = (P(None, None, "gx", "gy", "gz"), P(None, None, "gx", "gy", "gz"), P(), P())
    return jax.shard_map(shards, mesh=mesh, in_specs=in_specs, out_specs=out_specs, check_vma=False)
```

profile of v0, /device:TPU:0, one launch (start us, length us, event | category | flops | bytes accessed | tf_op | source)
XLA Modules:
  0.0 385.9 jit_solution(2596643986068705321)
XLA Ops:
  2.5 4.8 %collective-permute-start = (f32[11,2,8,128]{3,2,1,0:T(8,128)S(1)}, f32[11,2,8,128]{3,2,1,0:T(8,128)S(1)}, u32[]{:S(2)}, u32[]{:S(2)}) collective-permute-start(f32[11,2,8,128]{3,2,1,0:T(8,128)S(1)} %pad_maximum_fusion.10), channel_id=1, source_target_pairs={{0,8},{8,16},{16,24},{1,9},{9,17},{17,25},{2,10},{10,18},{18,26},{... | collective-permute-start | bytes 270344 | tf_op jit(solution)/shard_map/ppermute | solution.py:18
  7.4 1.3 collective-permute-start.1
  9.9 4.6 %collective-permute-start.6 = (f32[3,8,1,8,128]{4,1,3,2,0:T(8,128)S(1)}, f32[3,8,1,8,128]{4,1,3,2,0:T(8,128)S(1)}, u32[]{:S(2)}, u32[]{:S(2)}) collective-permute-start(f32[3,8,1,8,128]{4,1,3,2,0:T(8,128)S(1)} %copy.383), channel_id=1, source_target_pairs={{0,8},{8,16},{16,24},{1,9},{9,17},{17,25},{2,10},{10,18},{18,26},{... | collective-permute-start | bytes 294920 | tf_op jit(solution)/shard_map/ppermute | solution.py:18
  14.5 1.3 collective-permute-start.7
  16.7 4.8 %collective-permute-done.7 = f32[3,8,1,8,128]{4,1,3,2,0:T(8,128)S(1)} collective-permute-done((f32[3,8,1,8,128]{4,1,3,2,0:T(8,128)S(1)}, f32[3,8,1,8,128]{4,1,3,2,0:T(8,128)S(1)}, u32[]{:S(2)}, u32[]{:S(2)}) %collective-permute-start.7) | collective-permute-done | bytes 98336 | tf_op jit(solution)/shard_map/ppermute | solution.py:21
  21.6 1.3 collective-permute-start.8
  22.9 1.3 collective-permute-start.9
  24.2 1.8 collective-permute-done.9
  27.1 3.5 collective-permute-start.10
  30.7 1.3 collective-permute-start.11
  32.0 3.8 copy.222
  35.8 2.4 collective-permute-start.2
  38.9 1.3 collective-permute-start.3
  40.2 1.5 collective-permute-done.10
  42.5 3.3 collective-permute-done.11
  45.9 1.6 pad_maximum_fusion.1
  47.5 4.5 %copy.221 = f32[11,6,2,128]{2,1,3,0:T(8,128)} copy(f32[11,6,2,128]{3,1,2,0:T(8,128)} %collective-permute-done.2) | data formatting | bytes 135168 | tf_op jit(solution)/shard_map/ppermute | solution.py:18
  52.0 3.9 %copy.223 = f32[11,6,2,128]{2,1,3,0:T(8,128)} copy(f32[11,6,2,128]{3,1,2,0:T(8,128)S(1)} %collective-permute-done.3) | data formatting | bytes 135168 | tf_op jit(solution)/shard_map/ppermute | solution.py:21
  55.9 9.0 %pad_maximum_fusion = f32[11,6,12,128]{2,1,3,0:T(8,128)S(1)} fusion(f32[11,6,2,128]{2,1,3,0:T(8,128)} %copy.223, f32[11,6,8,128]{2,1,3,0:T(8,128)} %copy.222, f32[11,6,2,128]{2,1,3,0:T(8,128)} %copy.221), kind=kLoop, calls=%fused_computation | loop fusion | flops 202752 | bytes 811008 | tf_op jit(solution)/shard_map/concatenate | solution.py:22
  65.0 2.5 copy-done.1
  67.5 3.5 collective-permute-start.4
  70.9 1.3 collective-permute-start.5
  73.2 4.2 %copy.225 = f32[11,6,12,128]{3,2,1,0:T(8,128)S(1)} copy(f32[11,6,12,128]{2,1,3,0:T(8,128)} %copy-done.1) | data formatting | bytes 811008 | tf_op jit(solution)/shard_map/concatenate | solution.py:22
  77.9 1.3 copy.226
  80.4 1.4 fusion.187
  81.9 1.4 fusion.175
  84.0 4.7 %collective-permute-start.12 = (f32[3,8,1,8,128]{4,1,3,2,0:T(8,128)S(1)}, f32[3,8,1,8,128]{4,1,3,2,0:T(8,128)S(1)}, u32[]{:S(2)}, u32[]{:S(2)}) collective-permute-start(f32[3,8,1,8,128]{4,1,3,2,0:T(8,128)S(1)} %get-tuple-element.86), channel_id=1, source_target_pairs={{0,8},{8,16},{16,24},{1,9},{9,17},{17,25},{2,10},{10,18},{18,26},{... | collective-permute-start | bytes 294920 | tf_op jit(solution)/shard_map/ppermute | solution.py:18
  88.7 1.3 collective-permute-start.13
  90.9 4.3 %collective-permute-done.13 = f32[3,8,1,8,128]{4,1,3,2,0:T(8,128)S(1)} collective-permute-done((f32[3,8,1,8,128]{4,1,3,2,0:T(8,128)S(1)}, f32[3,8,1,8,128]{4,1,3,2,0:T(8,128)S(1)}, u32[]{:S(2)}, u32[]{:S(2)}) %collective-permute-start.13) | collective-permute-done | bytes 98336 | tf_op jit(solution)/shard_map/ppermute | solution.py:21
  95.2 1.3 collective-permute-start.14
  96.5 1.3 collective-permute-start.15
  97.8 1.8 collective-permute-done.15
  99.9 4.6 %collective-permute-start.16 = (f32[3,8,4,10,1]{4,1,3,2,0:T(8,128)S(1)}, f32[3,8,4,10,1]{4,1,3,2,0:T(8,128)S(1)}, u32[]{:S(2)}, u32[]{:S(2)}) collective-permute-start(f32[3,8,4,10,1]{4,1,3,2,0:T(8,128)S(1)} %get-tuple-element.68), channel_id=1, source_target_pairs={{0,1},{1,2},{2,3},{4,5},{5,6},{6,7},{8,9},{9,10},{10,11},{12,13},{... | collective-permute-start | bytes 11528 | tf_op jit(solution)/shard_map/ppermute | solution.py:18
  104.5 1.3 collective-permute-start.17
  105.8 9.5 %collective-permute-done.16 = f32[3,8,4,10,1]{4,1,3,2,0:T(8,128)S(1)} collective-permute-done((f32[3,8,4,10,1]{4,1,3,2,0:T(8,128)S(1)}, f32[3,8,4,10,1]{4,1,3,2,0:T(8,128)S(1)}, u32[]{:S(2)}, u32[]{:S(2)}) %collective-permute-start.16) | collective-permute-done | bytes 3872 | tf_op jit(solution)/shard_map/ppermute | solution.py:18
  115.2 4.1 %collective-permute-done.17 = f32[3,8,4,10,1]{4,1,3,2,0:T(8,128)S(1)} collective-permute-done((f32[3,8,4,10,1]{4,1,3,2,0:T(8,128)S(1)}, f32[3,8,4,10,1]{4,1,3,2,0:T(8,128)S(1)}, u32[]{:S(2)}, u32[]{:S(2)}) %collective-permute-start.17) | collective-permute-done | bytes 3872 | tf_op jit(solution)/shard_map/ppermute | solution.py:21
  120.6 2.8 collective-permute-start.18
  123.4 1.3 collective-permute-start.19
  125.6 4.3 %collective-permute-done.19 = f32[3,8,1,8,128]{4,1,3,2,0:T(8,128)S(1)} collective-permute-done((f32[3,8,1,8,128]{4,1,3,2,0:T(8,128)S(1)}, f32[3,8,1,8,128]{4,1,3,2,0:T(8,128)S(1)}, u32[]{:S(2)}, u32[]{:S(2)}) %collective-permute-start.19) | collective-permute-done | bytes 98336 | tf_op jit(solution)/shard_map/ppermute | solution.py:21
  130.0 1.3 collective-permute-start.20
  131.3 1.3 collective-permute-start.21
  132.6 1.8 collective-permute-done.21
  134.6 3.5 collective-permute-start.22
  138.1 1.5 collective-permute-start.23
  139.6 9.3 %collective-permute-done.22 = f32[3,8,4,10,1]{4,1,3,2,0:T(8,128)S(1)} collective-permute-done((f32[3,8,4,10,1]{4,1,3,2,0:T(8,128)S(1)}, f32[3,8,4,10,1]{4,1,3,2,0:T(8,128)S(1)}, u32[]{:S(2)}, u32[]{:S(2)}) %collective-permute-start.22) | collective-permute-done | bytes 3872 | tf_op jit(solution)/shard_map/ppermute | solution.py:18
  148.9 4.1 %collective-permute-done.23 = f32[3,8,4,10,1]{4,1,3,2,0:T(8,128)S(1)} collective-permute-done((f32[3,8,4,10,1]{4,1,3,2,0:T(8,128)S(1)}, f32[3,8,4,10,1]{4,1,3,2,0:T(8,128)S(1)}, u32[]{:S(2)}, u32[]{:S(2)}) %collective-permute-start.23) | collective-permute-done | bytes 3872 | tf_op jit(solution)/shard_map/ppermute | solution.py:21
  154.3 2.8 collective-permute-start.24
  157.1 1.3 collective-permute-start.25
  159.3 4.3 %collective-permute-done.25 = f32[3,8,1,8,128]{4,1,3,2,0:T(8,128)S(1)} collective-permute-done((f32[3,8,1,8,128]{4,1,3,2,0:T(8,128)S(1)}, f32[3,8,1,8,128]{4,1,3,2,0:T(8,128)S(1)}, u32[]{:S(2)}, u32[]{:S(2)}) %collective-permute-start.25) | collective-permute-done | bytes 98336 | tf_op jit(solution)/shard_map/ppermute | solution.py:21
  163.6 1.3 collective-permute-start.26
  164.9 1.3 collective-permute-start.27
  166.5 1.5 collective-permute-done.27
  168.3 2.2 collective-permute-start.28
  170.5 1.3 collective-permute-start.29
  172.1 9.1 %collective-permute-done.28 = f32[3,8,4,10,1]{4,1,3,2,0:T(8,128)S(1)} collective-permute-done((f32[3,8,4,10,1]{4,1,3,2,0:T(8,128)S(1)}, f32[3,8,4,10,1]{4,1,3,2,0:T(8,128)S(1)}, u32[]{:S(2)}, u32[]{:S(2)}) %collective-permute-start.28) | collective-permute-done | bytes 3872 | tf_op jit(solution)/shard_map/ppermute | solution.py:18
  181.2 4.1 %collective-permute-done.29 = f32[3,8,4,10,1]{4,1,3,2,0:T(8,128)S(1)} collective-permute-done((f32[3,8,4,10,1]{4,1,3,2,0:T(8,128)S(1)}, f32[3,8,4,10,1]{4,1,3,2,0:T(8,128)S(1)}, u32[]{:S(2)}, u32[]{:S(2)}) %collective-permute-start.29) | collective-permute-done | bytes 3872 | tf_op jit(solution)/shard_map/ppermute | solution.py:21
  186.8 38.2 %all-reduce.3 = (f32[128,8]{0,1:T(8,128)S(1)}, f32[128,8]{0,1:T(8,128)S(1)}, f32[128,8]{0,1:T(8,128)S(1)}, f32[128,8]{0,1:T(8,128)S(1)}) all-reduce(f32[128,8]{0,1:T(8,128)S(1)} %fusion.25, f32[128,8]{0,1:T(8,128)S(1)} %fusion.13, f32[128,8]{0,1:T(8,128)S(1)} %fusion.17, ...), channel_id=1, replica_groups=mesh['gx'=4,'gy'=2,'gz'=4] {'gx','gy','gz'}, use_global_device_ids=true, to_apply=%region_0.0 | all-reduce | flops 4096 | bytes 32768 | tf_op jit(solution)/shard_map/psum | solution.py:81
  229.2 40.9 %all-reduce.2 = (f32[8,8]{0,1:T(8,128)S(1)}, f32[8,8]{0,1:T(8,128)S(1)}, f32[8,8]{0,1:T(8,128)S(1)}, f32[8,8]{0,1:T(8,128)S(1)}) all-reduce(f32[8,8]{0,1:T(8,128)S(1)} %fusion.33, f32[8,8]{0,1:T(8,128)S(1)} %fusion.29, f32[8,8]{0,1:T(8,128)S(1)} %fusion.30, f32[8,8]{0,1:T(8,128)S(1)} %fusion.31), channel_id=1, replica_groups=mesh['gx'=4,'gy'=2,'gz'=4] {'gx','gy','gz'}, use_global_device_ids=true, to_apply=%region_1.0 | all-reduce | flops 256 | bytes 2048 | tf_op jit(solution)/shard_map/psum | solution.py:83
  284.5 39.8 %all-reduce.1 = (f32[128,8]{0,1:T(8,128)S(1)}, f32[128,8]{0,1:T(8,128)S(1)}, f32[128,8]{0,1:T(8,128)S(1)}, f32[128,8]{0,1:T(8,128)S(1)}) all-reduce(f32[128,8]{0,1:T(8,128)S(1)} %fusion.23, f32[128,8]{0,1:T(8,128)S(1)} %fusion.11, f32[128,8]{0,1:T(8,128)S(1)} %fusion.15, ...), channel_id=1, replica_groups=mesh['gx'=4,'gy'=2,'gz'=4] {'gx','gy','gz'}, use_global_device_ids=true, to_apply=%region_4.0 | all-reduce | flops 4096 | bytes 32768 | tf_op jit(solution)/shard_map/psum | solution.py:86
  328.5 40.9 %all-reduce = (f32[8,8]{0,1:T(8,128)S(1)}, f32[8,8]{0,1:T(8,128)S(1)}, f32[8,8]{0,1:T(8,128)S(1)}, f32[8,8]{0,1:T(8,128)S(1)}) all-reduce(f32[8,8]{0,1:T(8,128)S(1)} %fusion.32, f32[8,8]{0,1:T(8,128)S(1)} %fusion.26, f32[8,8]{0,1:T(8,128)S(1)} %fusion.27, f32[8,8]{0,1:T(8,128)S(1)} %fusion.28), channel_id=1, replica_groups=mesh['gx'=4,'gy'=2,'gz'=4] {'gx','gy','gz'}, use_global_device_ids=true, to_apply=%region_5.0 | all-reduce | flops 256 | bytes 2048 | tf_op jit(solution)/shard_map/psum | solution.py:90
  370.9 1.5 convolution_bitcast_fusion.16
  374.7 1.5 convolution_bitcast_fusion.19
  377.6 1.5 convolution_bitcast_fusion.18
  380.6 1.5 convolution_bitcast_fusion.17
  (176 shorter events, 51.0 us)
Async XLA Ops:
  0.6 8.0 %copy-start = (bf16[2,3,8,128,128]{4,3,2,1,0:T(8,128)(2,1)S(1)}, bf16[2,3,8,128,128]{4,3,2,1,0:T(8,128)(2,1)}, u32[]{:S(2)}) copy-start(bf16[2,3,8,128,128]{4,3,2,1,0:T(8,128)(2,1)} %param.10) | copy-start | bytes 4718596
  2.5 21.7 %collective-permute-start = (f32[11,2,8,128]{3,2,1,0:T(8,128)S(1)}, f32[11,2,8,128]{3,2,1,0:T(8,128)S(1)}, u32[]{:S(2)}, u32[]{:S(2)}) collective-permute-start(f32[11,2,8,128]{3,2,1,0:T(8,128)S(1)} %pad_maximum_fusion.10), channel_id=1, source_target_pairs={{0,8},{8,16},{16,24},{1,9},{9,17},{17,25},{2,10},{10,18},{18,26},{... | collective-permute-start | bytes 270344 | tf_op jit(solution)/shard_map/ppermute | solution.py:18
  7.4 16.8 %collective-permute-start.1 = (f32[11,2,8,128]{3,2,1,0:T(8,128)S(1)}, f32[11,2,8,128]{3,2,1,0:T(8,128)S(1)}, u32[]{:S(2)}, u32[]{:S(2)}) collective-permute-start(f32[11,2,8,128]{3,2,1,0:T(8,128)S(1)} %pad_maximum_fusion.10), channel_id=1, source_target_pairs={{8,0},{16,8},{24,16},{9,1},{17,9},{25,17},{10,2},{18,10},{26,18},{... | collective-permute-start | bytes 270344 | tf_op jit(solution)/shard_map/ppermute | solution.py:21
  9.9 6.8 %collective-permute-start.6 = (f32[3,8,1,8,128]{4,1,3,2,0:T(8,128)S(1)}, f32[3,8,1,8,128]{4,1,3,2,0:T(8,128)S(1)}, u32[]{:S(2)}, u32[]{:S(2)}) collective-permute-start(f32[3,8,1,8,128]{4,1,3,2,0:T(8,128)S(1)} %copy.383), channel_id=1, source_target_pairs={{0,8},{8,16},{16,24},{1,9},{9,17},{17,25},{2,10},{10,18},{18,26},{... | collective-permute-start | bytes 294920 | tf_op jit(solution)/shard_map/ppermute | solution.py:18
  14.5 7.0 %collective-permute-start.7 = (f32[3,8,1,8,128]{4,1,3,2,0:T(8,128)S(1)}, f32[3,8,1,8,128]{4,1,3,2,0:T(8,128)S(1)}, u32[]{:S(2)}, u32[]{:S(2)}) collective-permute-start(f32[3,8,1,8,128]{4,1,3,2,0:T(8,128)S(1)} %copy.384), channel_id=1, source_target_pairs={{8,0},{16,8},{24,16},{9,1},{17,9},{25,17},{10,2},{18,10},{26,18},{... | collective-permute-start | bytes 294920 | tf_op jit(solution)/shard_map/ppermute | solution.py:21
  21.6 2.7 collective-permute-start.8
  22.9 3.1 collective-permute-start.9
  27.1 14.6 %collective-permute-start.10 = (f32[3,8,4,10,1]{4,1,3,2,0:T(8,128)}, f32[3,8,4,10,1]{4,1,3,2,0:T(8,128)S(1)}, u32[]{:S(2)}, u32[]{:S(2)}) collective-permute-start(f32[3,8,4,10,1]{4,1,3,2,0:T(8,128)} %get-tuple-element.70), channel_id=1, source_target_pairs={{0,1},{1,2},{2,3},{4,5},{5,6},{6,7},{8,9},{9,10},{10,11},{12,13},{... | collective-permute-start | bytes 11528 | tf_op jit(solution)/shard_map/ppermute | solution.py:18
  30.7 15.2 %collective-permute-start.11 = (f32[3,8,4,10,1]{4,1,3,2,0:T(8,128)}, f32[3,8,4,10,1]{4,1,3,2,0:T(8,128)}, u32[]{:S(2)}, u32[]{:S(2)}) collective-permute-start(f32[3,8,4,10,1]{4,1,3,2,0:T(8,128)} %get-tuple-element.71), channel_id=1, source_target_pairs={{1,0},{2,1},{3,2},{5,4},{6,5},{7,6},{9,8},{10,9},{11,10},{13,12},{... | collective-permute-start | bytes 11528 | tf_op jit(solution)/shard_map/ppermute | solution.py:21
  35.8 11.7 %collective-permute-start.2 = (f32[11,6,2,128]{3,1,2,0:T(8,128)S(1)}, f32[11,6,2,128]{3,1,2,0:T(8,128)}, u32[]{:S(2)}, u32[]{:S(2)}) collective-permute-start(f32[11,6,2,128]{3,1,2,0:T(8,128)S(1)} %copy.326), channel_id=1, source_target_pairs={{0,4},{1,5},{2,6},{3,7},{8,12},{9,13},{10,14},{11,15},{16,20},{17,... | collective-permute-start | bytes 202760 | tf_op jit(solution)/shard_map/ppermute | solution.py:18
  38.9 13.1 %collective-permute-start.3 = (f32[11,6,2,128]{3,1,2,0:T(8,128)}, f32[11,6,2,128]{3,1,2,0:T(8,128)S(1)}, u32[]{:S(2)}, u32[]{:S(2)}) collective-permute-start(f32[11,6,2,128]{3,1,2,0:T(8,128)} %copy.327), channel_id=1, source_target_pairs={{4,0},{5,1},{6,2},{7,3},{12,8},{13,9},{14,10},{15,11},{20,16},{21,... | collective-permute-start | bytes 202760 | tf_op jit(solution)/shard_map/ppermute | solution.py:21
  41.7 0.8 copy-start.2
  65.0 2.5 copy-start.1
  67.5 9.9 %collective-permute-start.4 = (f32[11,6,12,2]{2,1,3,0:T(8,128)S(1)}, f32[11,6,12,2]{2,1,3,0:T(8,128)S(1)}, u32[]{:S(2)}, u32[]{:S(2)}) collective-permute-start(f32[11,6,12,2]{2,1,3,0:T(8,128)S(1)} %get-tuple-element.44), channel_id=1, source_target_pairs={{0,1},{1,2},{2,3},{4,5},{5,6},{6,7},{8,9},{9,10},{10,11},{12,13},{... | collective-permute-start | bytes 19016 | tf_op jit(solution)/shard_map/ppermute | solution.py:18
  70.9 7.0 %collective-permute-start.5 = (f32[11,6,12,2]{2,1,3,0:T(8,128)S(1)}, f32[11,6,12,2]{2,1,3,0:T(8,128)S(1)}, u32[]{:S(2)}, u32[]{:S(2)}) collective-permute-start(f32[11,6,12,2]{2,1,3,0:T(8,128)S(1)} %get-tuple-element.45), channel_id=1, source_target_pairs={{1,0},{2,1},{3,2},{5,4},{6,5},{7,6},{9,8},{10,9},{11,10},{13,12},{... | collective-permute-start | bytes 19016 | tf_op jit(solution)/shard_map/ppermute | solution.py:21
  79.2 4.2 %copy-start.3 = (f32[3,8]{1,0:T(4,128)S(1)}, f32[3,8]{1,0:T(4,128)}, u32[]{:S(2)}) copy-start(f32[3,8]{1,0:T(4,128)} %param.16) | copy-start | bytes 292
  79.2 4.3 %copy-start.4 = (bf16[128,8]{0,1:T(8,128)(2,1)S(1)}, bf16[128,8]{0,1:T(8,128)(2,1)}, u32[]{:S(2)}) copy-start(bf16[128,8]{0,1:T(8,128)(2,1)} %param.12) | copy-start | bytes 6148
  84.0 6.9 %collective-permute-start.12 = (f32[3,8,1,8,128]{4,1,3,2,0:T(8,128)S(1)}, f32[3,8,1,8,128]{4,1,3,2,0:T(8,128)S(1)}, u32[]{:S(2)}, u32[]{:S(2)}) collective-permute-start(f32[3,8,1,8,128]{4,1,3,2,0:T(8,128)S(1)} %get-tuple-element.86), channel_id=1, source_target_pairs={{0,8},{8,16},{16,24},{1,9},{9,17},{17,25},{2,10},{10,18},{18,26},{... | collective-permute-start | bytes 294920 | tf_op jit(solution)/shard_map/ppermute | solution.py:18
  88.7 6.5 %collective-permute-start.13 = (f32[3,8,1,8,128]{4,1,3,2,0:T(8,128)S(1)}, f32[3,8,1,8,128]{4,1,3,2,0:T(8,128)S(1)}, u32[]{:S(2)}, u32[]{:S(2)}) collective-permute-start(f32[3,8,1,8,128]{4,1,3,2,0:T(8,128)S(1)} %get-tuple-element.87), channel_id=1, source_target_pairs={{8,0},{16,8},{24,16},{9,1},{17,9},{25,17},{10,2},{18,10},{26,18},{... | collective-permute-start | bytes 294920 | tf_op jit(solution)/shard_map/ppermute | solution.py:21
  95.2 2.6 collective-permute-start.14
  96.5 3.1 collective-permute-start.15
  99.9 15.3 %collective-permute-start.16 = (f32[3,8,4,10,1]{4,1,3,2,0:T(8,128)S(1)}, f32[3,8,4,10,1]{4,1,3,2,0:T(8,128)S(1)}, u32[]{:S(2)}, u32[]{:S(2)}) collective-permute-start(f32[3,8,4,10,1]{4,1,3,2,0:T(8,128)S(1)} %get-tuple-element.68), channel_id=1, source_target_pairs={{0,1},{1,2},{2,3},{4,5},{5,6},{6,7},{8,9},{9,10},{10,11},{12,13},{... | collective-permute-start | bytes 11528 | tf_op jit(solution)/shard_map/ppermute | solution.py:18
  104.5 14.9 %collective-permute-start.17 = (f32[3,8,4,10,1]{4,1,3,2,0:T(8,128)S(1)}, f32[3,8,4,10,1]{4,1,3,2,0:T(8,128)S(1)}, u32[]{:S(2)}, u32[]{:S(2)}) collective-permute-start(f32[3,8,4,10,1]{4,1,3,2,0:T(8,128)S(1)} %get-tuple-element.69), channel_id=1, source_target_pairs={{1,0},{2,1},{3,2},{5,4},{6,5},{7,6},{9,8},{10,9},{11,10},{13,12},{... | collective-permute-start | bytes 11528 | tf_op jit(solution)/shard_map/ppermute | solution.py:21
  120.6 5.0 %collective-permute-start.18 = (f32[3,8,1,8,128]{4,1,3,2,0:T(8,128)S(1)}, f32[3,8,1,8,128]{4,1,3,2,0:T(8,128)S(1)}, u32[]{:S(2)}, u32[]{:S(2)}) collective-permute-start(f32[3,8,1,8,128]{4,1,3,2,0:T(8,128)S(1)} %copy.385), channel_id=1, source_target_pairs={{0,8},{8,16},{16,24},{1,9},{9,17},{17,25},{2,10},{10,18},{18,26},{... | collective-permute-start | bytes 294920 | tf_op jit(solution)/shard_map/ppermute | solution.py:18
  123.4 6.5 %collective-permute-start.19 = (f32[3,8,1,8,128]{4,1,3,2,0:T(8,128)S(1)}, f32[3,8,1,8,128]{4,1,3,2,0:T(8,128)S(1)}, u32[]{:S(2)}, u32[]{:S(2)}) collective-permute-start(f32[3,8,1,8,128]{4,1,3,2,0:T(8,128)S(1)} %copy.386), channel_id=1, source_target_pairs={{8,0},{16,8},{24,16},{9,1},{17,9},{25,17},{10,2},{18,10},{26,18},{... | collective-permute-start | bytes 294920 | tf_op jit(solution)/shard_map/ppermute | solution.py:21
  130.0 2.6 collective-permute-start.20
  131.3 3.1 collective-permute-start.21
  134.6 14.2 %collective-permute-start.22 = (f32[3,8,4,10,1]{4,1,3,2,0:T(8,128)S(1)}, f32[3,8,4,10,1]{4,1,3,2,0:T(8,128)S(1)}, u32[]{:S(2)}, u32[]{:S(2)}) collective-permute-start(f32[3,8,4,10,1]{4,1,3,2,0:T(8,128)S(1)} %get-tuple-element.66), channel_id=1, source_target_pairs={{0,1},{1,2},{2,3},{4,5},{5,6},{6,7},{8,9},{9,10},{10,11},{12,13},{... | collective-permute-start | bytes 11528 | tf_op jit(solution)/shard_map/ppermute | solution.py:18
  138.1 14.9 %collective-permute-start.23 = (f32[3,8,4,10,1]{4,1,3,2,0:T(8,128)S(1)}, f32[3,8,4,10,1]{4,1,3,2,0:T(8,128)S(1)}, u32[]{:S(2)}, u32[]{:S(2)}) collective-permute-start(f32[3,8,4,10,1]{4,1,3,2,0:T(8,128)S(1)} %get-tuple-element.67), channel_id=1, source_target_pairs={{1,0},{2,1},{3,2},{5,4},{6,5},{7,6},{9,8},{10,9},{11,10},{13,12},{... | collective-permute-start | bytes 11528 | tf_op jit(solution)/shard_map/ppermute | solution.py:21
  154.3 5.0 %collective-permute-start.24 = (f32[3,8,1,8,128]{4,1,3,2,0:T(8,128)S(1)}, f32[3,8,1,8,128]{4,1,3,2,0:T(8,128)S(1)}, u32[]{:S(2)}, u32[]{:S(2)}) collective-permute-start(f32[3,8,1,8,128]{4,1,3,2,0:T(8,128)S(1)} %get-tuple-element.82), channel_id=1, source_target_pairs={{0,8},{8,16},{16,24},{1,9},{9,17},{17,25},{2,10},{10,18},{18,26},{... | collective-permute-start | bytes 294920 | tf_op jit(solution)/shard_map/ppermute | solution.py:18
  157.1 6.5 %collective-permute-start.25 = (f32[3,8,1,8,128]{4,1,3,2,0:T(8,128)S(1)}, f32[3,8,1,8,128]{4,1,3,2,0:T(8,128)S(1)}, u32[]{:S(2)}, u32[]{:S(2)}) collective-permute-start(f32[3,8,1,8,128]{4,1,3,2,0:T(8,128)S(1)} %get-tuple-element.83), channel_id=1, source_target_pairs={{8,0},{16,8},{24,16},{9,1},{17,9},{25,17},{10,2},{18,10},{26,18},{... | collective-permute-start | bytes 294920 | tf_op jit(solution)/shard_map/ppermute | solution.py:21
  163.6 2.9 collective-permute-start.26
  164.9 3.1 collective-permute-start.27
  168.3 13.0 %collective-permute-start.28 = (f32[3,8,4,10,1]{4,1,3,2,0:T(8,128)S(1)}, f32[3,8,4,10,1]{4,1,3,2,0:T(8,128)S(1)}, u32[]{:S(2)}, u32[]{:S(2)}) collective-permute-start(f32[3,8,4,10,1]{4,1,3,2,0:T(8,128)S(1)} %get-tuple-element.64), channel_id=1, source_target_pairs={{0,1},{1,2},{2,3},{4,5},{5,6},{6,7},{8,9},{9,10},{10,11},{12,13},{... | collective-permute-start | bytes 11528 | tf_op jit(solution)/shard_map/ppermute | solution.py:18
  170.5 14.9 %collective-permute-start.29 = (f32[3,8,4,10,1]{4,1,3,2,0:T(8,128)S(1)}, f32[3,8,4,10,1]{4,1,3,2,0:T(8,128)S(1)}, u32[]{:S(2)}, u32[]{:S(2)}) collective-permute-start(f32[3,8,4,10,1]{4,1,3,2,0:T(8,128)S(1)} %get-tuple-element.65), channel_id=1, source_target_pairs={{1,0},{2,1},{3,2},{5,4},{6,5},{7,6},{9,8},{10,9},{11,10},{13,12},{... | collective-permute-start | bytes 11528 | tf_op jit(solution)/shard_map/ppermute | solution.py:21
where the time goes:
time: 388 us; the launch traced here: 386 us
  blocking collectives  160 us (41%)
  waiting for transfers between devices  73 us (19%)
  starting transfers between devices  64.1 us (17%)
  other arithmetic  38.1 us (10%)
  local copies, waits for them, and re-layouts  27.4 us (7%)
  matrix products  22 us (6%)
    ppermute x15, starting transfers between devices, padded_2(): lax.ppermute(lax.slice_in_dim(block, block.shape[dim] - width, None, axis...  44.5 us
    psum x1, blocking collectives, orthonormalize(): lax.psum(local_gram(first_resid) * dof_weight, ('gx', 'gy', 'gz'))  40.9 us
    psum x1, blocking collectives, orthonormalize(): lax.psum(local_gram(second_resid) * dof_weight, ('gx', 'gy', 'gz'))  40.9 us
    ppermute x15, waiting for transfers between devices, padded_2(): lax.ppermute(lax.slice_in_dim(block, 0, width, axis=dim), axis, backward)  40.5 us
    psum x1, blocking collectives, orthonormalize(): lax.psum(project(basis, first_q.astype(jnp.bfloat16)) * dof_weight, ('gx'...  39.8 us
    psum x1, blocking collectives, orthonormalize(): first_coef = lax.psum(partial_coef, ('gx', 'gy', 'gz'))  38.2 us
    ppermute x15, waiting for transfers between devices, padded_2(): lax.ppermute(lax.slice_in_dim(block, block.shape[dim] - width, None, axis...  32.6 us
    ppermute x15, starting transfers between devices, padded_2(): lax.ppermute(lax.slice_in_dim(block, 0, width, axis=dim), axis, backward)  19.6 us
  transfers between devices with their start and end apart: 30, of which 20 were waited for; matrix products, arithmetic and copies ran while one was open for 5% of the time, Pallas kernels for 0%

commit v1 on v0

v1 whole, which is shorter than its diff:
```python
import functools
import jax
import jax.numpy as jnp
from jax import lax
from jax.experimental import pallas as pl
from jax.experimental.pallas import tpu as pltpu
from jax.sharding import PartitionSpec as P

STEPS = 4
MESH_IDS = pl.DeviceIdType.MESH
AXES = ("gx", "gy", "gz")
HIGHEST = lax.Precision.HIGHEST
NT = (((1,), (1,)), ((), ()))
NN = (((1,), (0,)), ((), ()))
TN = (((0,), (0,)), ((), ()))

step_squared = 0.1
ramp_steps = 4.0


def dot32(a, b, dims):
    return lax.dot_general(a, b, dims, precision=HIGHEST, preferred_element_type=jnp.float32)


def dot16(a, b, dims):
    return lax.dot_general(a, b, dims, preferred_element_type=jnp.float32)


def small_product(a, b):
    total = a[:, :, 0:1] * b[:, 0:1, :]
    for k in range(1, b.shape[1]):
        total = total + a[:, :, k : k + 1] * b[:, k : k + 1, :]
    return total


def factor(gram):
    s, n, _ = gram.shape
    rows = lax.broadcasted_iota(jnp.int32, (s, n, 128), 1)
    lanes = lax.broadcasted_iota(jnp.int32, (s, n, 128), 2)
    work = jnp.concatenate([gram, jnp.zeros((s, n, 128 - n), jnp.float32)], axis=2)
    work = jnp.where(lanes == rows + n, 1.0, work)
    pivots = jnp.ones((s, n, 128), jnp.float32)
    for k in range(n):
        pivot = work[:, k : k + 1, k : k + 1]
        pivots = jnp.where(rows == k, pivot, pivots)
        if k < n - 1:
            ratio = jnp.where(rows > k, work[:, :, k : k + 1] / pivot, 0.0)
            work = work - ratio * work[:, k : k + 1, :]
    work = work * lax.rsqrt(pivots)
    upper = jnp.where(lanes >= rows, work, 0.0)[:, :, :n]
    return upper, work[:, :, n : 2 * n]


def kernel(sizes, basis_ref, now_ref, prev_ref, ids_ref, moduli_ref, mask_ref, drive_ref,
           disp_ref, modes_ref, coef_ref, rfac_ref,
           field_ref, ids_field_ref, hx_ref, hy_ref, hz_ref, zs_ref,
           ix_ref, iy_ref, iz_ref, izs_ref, coup_ref,
           gpart_ref, gy_buf, gx_buf, gz_buf, gslice_ref, gfull_ref,
           s0y, s0x, s0z, s1y, s1x, s1z, stat_ref,
           halo_send, halo_recv, g_send, g_recv, s_send, s_recv):
    nx, ny, nz = sizes
    count = dict(zip(AXES, sizes))
    me = {axis: lax.axis_index(axis) for axis in AXES}
    X, C, Y, Z, K = basis_ref.shape
    J = now_ref.shape[1]
    tiles = X * C * Y
    weight = 1.0 / (tiles * Z * nx * ny * nz)

    hx_ref[...] = jnp.zeros_like(hx_ref)
    hy_ref[...] = jnp.zeros_like(hy_ref)
    hz_ref[...] = jnp.zeros_like(hz_ref)
    ix_ref[...] = jnp.zeros_like(ix_ref)
    iy_ref[...] = jnp.zeros_like(iy_ref)
    iz_ref[...] = jnp.zeros_like(iz_ref)

    barrier = pltpu.get_barrier_semaphore()
    for axis in AXES:
        for d in range(1, count[axis]):
            pl.semaphore_signal(barrier, inc=1, device_id={axis: lax.rem(me[axis] + d, count[axis])},
                                device_id_type=MESH_IDS)
    pl.semaphore_wait(barrier, nx + ny + nz - 3)

    def halo_copies(slot, src, zsrc, dst_x, dst_y, dst_z):
        plan = []
        faces = {
            "gx": (src.at[X - 1], src.at[0], dst_x),
            "gy": (src.at[:, :, Y - 1], src.at[:, :, 0], dst_y),
            "gz": (zsrc.at[1], zsrc.at[0], dst_z),
        }
        for n_axis, axis in enumerate(AXES):
            up, down, dst = faces[axis]
            for side, face in ((0, up), (1, down)):
                target = me[axis] + (1 if side == 0 else -1)
                copy = pltpu.make_async_remote_copy(
                    src_ref=face, dst_ref=dst.at[side],
                    send_sem=halo_send.at[slot, 2 * n_axis + side],
                    recv_sem=halo_recv.at[slot, 2 * n_axis + side],
                    device_id={axis: target}, device_id_type=MESH_IDS)
                has_target = (me[axis] < count[axis] - 1) if side == 0 else (me[axis] > 0)
                has_source = (me[axis] > 0) if side == 0 else (me[axis] < count[axis] - 1)
                plan.append((has_target, has_source, copy))
        return plan

    def send_all(plan):
        for has_target, _, copy in plan:
            @pl.when(has_target)
            def _(copy=copy):
                copy.start()

    def recv_all(plan):
        for _, has_source, copy in plan:
            @pl.when(has_source)
            def _(copy=copy):
                copy.wait_recv()

    def drain(plan):
        for has_target, _, copy in plan:
            @pl.when(has_target)
            def _(copy=copy):
                copy.wait_send()

    def z_faces(value, zdst):
        turned = value.reshape(-1, Z).T
        zdst[0] = turned[0:8]
        zdst[1] = turned[Z - 8 : Z]

    def neighbours(value, hx, hy, hz):
        shape = value.shape
        x_lo = jnp.concatenate([hx[0][None], value[:-1]], axis=0)
        x_hi = jnp.concatenate([value[1:], hx[1][None]], axis=0)
        y_lo = jnp.concatenate([hy[0][:, :, None], value[:, :, :-1]], axis=2)
        y_hi = jnp.concatenate([value[:, :, 1:], hy[1][:, :, None]], axis=2)
        flat = value.reshape(-1, Z)
        lanes = lax.broadcasted_iota(jnp.int32, flat.shape, 1)
        turned = jnp.concatenate(
            [hz[1], jnp.zeros((Z - 16, flat.shape[0]), jnp.float32), hz[0]], axis=0).T
        z_lo = pltpu.roll(jnp.where(lanes == Z - 1, turned, flat), 1, 1)
        z_hi = pltpu.roll(jnp.where(lanes == 0, turned, flat), Z - 1, 1)
        return ((x_lo, x_hi), (y_lo, y_hi), (z_lo.reshape(shape), z_hi.reshape(shape)))

    def exchange(axis, src_of, dst_of, send_sem, recv_sem):
        started = []
        for d in range(1, count[axis]):
            peer = lax.rem(me[axis] + d, count[axis])
            started.append(pltpu.make_async_remote_copy(
                src_ref=src_of(peer), dst_ref=dst_of(me[axis]),
                send_sem=send_sem.at[d], recv_sem=recv_sem.at[d],
                device_id={axis: peer}, device_id_type=MESH_IDS))
        for copy in started:
            copy.start()
        return started

    def finish(started):
        for copy in started:
            copy.wait_recv()
            copy.wait_send()

    def total_of(buf):
        total = buf[0]
        for i in range(1, buf.shape[0]):
            total = total + buf[i]
        return total

    idf = (ids_ref[...] + 1).astype(jnp.float32)
    idf = jnp.broadcast_to(idf[:, None, :, None, :], (X, 1, Y, J, Z))
    ids_field_ref[...] = idf
    z_faces(idf, izs_ref)
    ids_plan = halo_copies(STEPS, ids_field_ref, izs_ref, ix_ref, iy_ref, iz_ref)
    send_all(ids_plan)

    basis = basis_ref[...].reshape(tiles * Z, K)
    both = jnp.concatenate([now_ref[...], prev_ref[...]], axis=1).astype(jnp.float32)
    both = both.T.astype(jnp.bfloat16)
    start = dot16(both, basis, NT)

    def as_field(flat):
        parts = [flat[:, t * Z : (t + 1) * Z] for t in range(tiles)]
        return jnp.stack(parts).reshape(X, C, Y, J, Z)

    def as_flat(value):
        parts = value.reshape(tiles, value.shape[-2], Z)
        return jnp.concatenate([parts[t] for t in range(tiles)], axis=1)

    field_ref[1] = as_field(start[:J])
    field_ref[0] = as_field(start[J:])
    z_faces(field_ref[1], zs_ref.at[0])
    plans = [halo_copies(s, field_ref.at[s + 1], zs_ref.at[s], hx_ref.at[s], hy_ref.at[s], hz_ref.at[s])
             for s in range(STEPS)]
    send_all(plans[0])

    rows = K // ny
    gpart_ref[...] = dot16(basis, basis, TN).reshape(ny, rows, K)
    gy_buf[me["gy"]] = gpart_ref[me["gy"]]
    g_stage = exchange("gy", lambda p: gpart_ref.at[p], lambda m: gy_buf.at[m],
                       g_send.at[0], g_recv.at[0])

    recv_all(ids_plan)
    def pick(p, index):
        value = jnp.zeros_like(index)
        for m in range(moduli_ref.shape[1]):
            value = jnp.where(index == float(m + 1), moduli_ref[p, m], value)
        return value
    around = neighbours(idf, ix_ref[...], iy_ref[...], iz_ref[...])
    scale = step_squared * pick(2, idf)
    for p in range(2):
        own = pick(p, idf)
        for a in range(3):
            for side in range(2):
                coup_ref[p, a, side] = (0.5 * scale * (own + pick(p, around[a][side])))[:, 0]
    sub = lax.broadcasted_iota(jnp.int32, (J, Z), 0)
    drives = []
    for c in range(C):
        column = jnp.zeros((J, Z), jnp.float32)
        for j in range(J):
            column = jnp.where(sub == j, drive_ref[c, j], column)
        drives.append(column)
    drives = jnp.stack(drives)[None, :, None]
    mask = jnp.stack([mask_ref[:, x, y, :] for x in range(X) for y in range(Y)])
    mask = mask.astype(jnp.float32).reshape(X, 1, Y, J, Z)
    load = scale * mask * drives

    stats = {}
    bufs = ((s0y, s0x, s0z), (s1y, s1x, s1z))

    def begin_pair(pair, snap):
        proj = dot16(snap, basis, NN)
        gram = dot16(snap, snap, NT)
        gram = jnp.concatenate([gram, jnp.zeros((2 * J, K - 2 * J), jnp.float32)], axis=1)
        return jnp.concatenate([proj, gram], axis=0) * weight

    def stat_start(pair, n_axis, value):
        buf = bufs[pair][n_axis]
        axis = ("gy", "gx", "gz")[n_axis]
        stat_ref[pair, n_axis] = value
        buf[me[axis]] = value
        return exchange(axis, lambda p: stat_ref.at[pair, n_axis], lambda m: buf.at[m],
                        s_send.at[pair, n_axis], s_recv.at[pair, n_axis])

    def stat_finish(pair, n_axis, started):
        finish(started)
        return total_of(bufs[pair][n_axis])

    snaps = []
    pending = None
    for step in range(STEPS):
        recv_all(plans[step])
        current = field_ref[step + 1]
        around = neighbours(current, hx_ref[step], hy_ref[step], hz_ref[step])
        ramp = min(1.0, (step + 1) / ramp_steps)
        following = 2.0 * current - field_ref[step] + ramp * load
        for a in range(3):
            for side in range(2):
                gap = current - around[a][side]
                kind = [coup_ref[0 if c == a else 1, a, side] for c in range(C)]
                following = following - jnp.stack(kind, axis=1) * gap
        if step < STEPS - 1:
            field_ref[step + 2] = following
            z_faces(following, zs_ref.at[step + 1])
            send_all(plans[step + 1])
        snaps.append(following)
        if step == 0:
            finish(g_stage)
            gslice_ref[0] = total_of(gy_buf)
            gx_buf[me["gx"]] = gslice_ref[0]
            g_stage = exchange("gx", lambda p: gslice_ref.at[0], lambda m: gx_buf.at[m],
                               g_send.at[1], g_recv.at[1])
        if step == 1:
            snap = as_flat(jnp.concatenate(snaps, axis=3).astype(jnp.bfloat16))
            pending = stat_start(0, 0, begin_pair(0, snap))
            finish(g_stage)
            gslice_ref[1] = total_of(gx_buf)
            gz_buf[me["gz"]] = gslice_ref[1]
            g_stage = exchange("gz", lambda p: gslice_ref.at[1], lambda m: gz_buf.at[m],
                               g_send.at[2], g_recv.at[2])
            snaps = []
        if step == 2:
            pending = stat_start(0, 1, stat_finish(0, 0, pending))
            finish(g_stage)
            gslice_ref[2] = total_of(gz_buf) * weight
            gfull_ref[me["gy"]] = gslice_ref[2]
            g_stage = exchange("gy", lambda p: gslice_ref.at[2], lambda m: gfull_ref.at[m],
                               g_send.at[3], g_recv.at[3])

    snap = as_flat(jnp.concatenate(snaps, axis=3).astype(jnp.bfloat16))
    late = stat_start(1, 0, begin_pair(1, snap))
    pending = stat_start(0, 2, stat_finish(0, 1, pending))
    last = snaps[1]
    flat_last = as_flat(last)
    for x in range(X):
        for c in range(C):
            for y in range(Y):
                disp_ref[c, :, x, y, :] = last[x, c, y]
    late = stat_start(1, 1, stat_finish(1, 0, late))
    finish(g_stage)
    gram_basis = gfull_ref[...].reshape(K, K)
    first = stat_finish(0, 2, pending)
    late = stat_start(1, 2, stat_finish(1, 1, late))
    second = stat_finish(1, 2, late)

    coef1 = jnp.concatenate([first[: 2 * J], second[: 2 * J]], axis=0)
    coef1_b = coef1.astype(jnp.bfloat16).astype(jnp.float32)
    def blocks(full):
        return jnp.stack([full[J * s : J * s + J, J * s : J * s + J] for s in range(full.shape[0] // J)])
    snap_gram = jnp.concatenate(
        [blocks(first[2 * J :, : 2 * J]), blocks(second[2 * J :, : 2 * J])], axis=0)
    left = coef1 - dot32(coef1_b, gram_basis, NN)
    gram1 = snap_gram - blocks(dot32(coef1_b, left, NT) + dot32(coef1, coef1_b, NT))
    upper1, inverse1 = factor(gram1)
    coef2 = small_product(inverse1, left.reshape(STEPS, J, K)).reshape(STEPS * J, K)
    coef2_b = coef2.astype(jnp.bfloat16).astype(jnp.float32)
    left2 = coef2 - dot32(coef2_b, gram_basis, NN)
    eye = (lax.broadcasted_iota(jnp.int32, (STEPS, J, J), 1)
           == lax.broadcasted_iota(jnp.int32, (STEPS, J, J), 2)).astype(jnp.float32)
    gram2 = eye - blocks(dot32(coef2_b, left2, NT) + dot32(coef2, coef2_b, NT))
    upper2, inverse2 = factor(gram2)
    rfac_ref[...] = small_product(upper2, upper1)
    for s in range(STEPS):
        coef_ref[s, 0] = coef1[J * s : J * s + J].T
        coef_ref[s, 1] = coef2[J * s : J * s + J].T

    inv1, inv2 = inverse1[STEPS - 1 :], inverse2[STEPS - 1 :]
    tail = slice(J * (STEPS - 1), J * STEPS)
    mix = small_product(inv1, coef1_b[tail][None]) + coef2_b[tail][None]
    mix = small_product(inv2, mix)[0]
    mix_hi = mix.astype(jnp.bfloat16).astype(jnp.float32)
    parts = jnp.concatenate([mix_hi, mix - mix_hi], axis=0).astype(jnp.bfloat16)
    spread = dot16(parts, basis, NT)
    rounded = flat_last.astype(jnp.bfloat16).astype(jnp.float32)
    modes = small_product(small_product(inv2, inv1), rounded[None])[0]
    modes = modes - (spread[:J] + spread[J:])
    t = 0
    for x in range(X):
        for c in range(C):
            for y in range(Y):
                modes_ref[c, :, x, y, :] = modes[:, t * Z : (t + 1) * Z]
                t += 1

    drain(ids_plan)
    for plan in plans:
        drain(plan)


def shards(sizes, basis, modal_now, modal_prev, material_ids, moduli, drive_mask, drive):
    nx, ny, nz = sizes
    X, C, Y, Z, K = basis.shape
    J = modal_now.shape[1]
    f32 = jnp.float32
    n_flat = X * C * Y * J
    vmem = pl.BlockSpec(memory_space=pltpu.VMEM)
    smem = pl.BlockSpec(memory_space=pltpu.SMEM)
    rows = K // ny
    srows = 4 * J
    most = max(sizes)
    return pl.pallas_call(
        functools.partial(kernel, sizes),
        out_shape=(
            jax.ShapeDtypeStruct((C, J, X, Y, Z), f32),
            jax.ShapeDtypeStruct((C, J, X, Y, Z), f32),
            jax.ShapeDtypeStruct((STEPS, 2, K, J), f32),
            jax.ShapeDtypeStruct((STEPS, J, J), f32),
        ),
        in_specs=[vmem, vmem, vmem, vmem, smem, vmem, smem],
        out_specs=(vmem, vmem, vmem, vmem),
        scratch_shapes=[
            pltpu.VMEM((STEPS + 1, X, C, Y, J, Z), f32),
            pltpu.VMEM((X, 1, Y, J, Z), f32),
            pltpu.VMEM((STEPS, 2, C, Y, J, Z), f32),
            pltpu.VMEM((STEPS, 2, X, C, J, Z), f32),
            pltpu.VMEM((STEPS, 2, 8, n_flat), f32),
            pltpu.VMEM((STEPS, 2, 8, n_flat), f32),
            pltpu.VMEM((2, 1, Y, J, Z), f32),
            pltpu.VMEM((2, X, 1, J, Z), f32),
            pltpu.VMEM((2, 8, X * Y * J), f32),
            pltpu.VMEM((2, 8, X * Y * J), f32),
            pltpu.VMEM((2, 3, 2, X, Y, J, Z), f32),
            pltpu.VMEM((ny, rows, K), f32),
            pltpu.VMEM((ny, rows, K), f32),
            pltpu.VMEM((nx, rows, K), f32),
            pltpu.VMEM((nz, rows, K), f32),
            pltpu.VMEM((3, rows, K), f32),
            pltpu.VMEM((ny, rows, K), f32),
        ] + [pltpu.VMEM((n, srows, K), f32) for _ in range(2) for n in (ny, nx, nz)] + [
            pltpu.VMEM((2, 3, srows, K), f32),
            pltpu.SemaphoreType.DMA((STEPS + 1, 6)),
            pltpu.SemaphoreType.DMA((STEPS + 1, 6)),
            pltpu.SemaphoreType.DMA((4, most)),
            pltpu.SemaphoreType.DMA((4, most)),
            pltpu.SemaphoreType.DMA((2, 3, most)),
            pltpu.SemaphoreType.DMA((2, 3, most)),
        ],
        compiler_params=pltpu.CompilerParams(
            collective_id=0, has_side_effects=True, vmem_limit_bytes=48 * 1024 * 1024),
        cost_estimate=pl.CostEstimate(flops=1000000000, bytes_accessed=3000000, transcendentals=0),
    )(basis, modal_now, modal_prev, material_ids, moduli, drive_mask, drive)


def solution(mesh):
    sizes = tuple(mesh.shape[axis] for axis in AXES)
    in_specs = (
        P("gx", None, "gy", "gz", None),
        P(),
        P(),
        P("gx", "gy", "gz"),
        P(),
        P(None, "gx", "gy", "gz"),
        P(),
    )
    out_specs = (P(None, None, "gx", "gy", "gz"), P(None, None, "gx", "gy", "gz"), P(), P())
    return jax.shard_map(functools.partial(shards, sizes), mesh=mesh, in_specs=in_specs,
                         out_specs=out_specs, check_vma=False)
```

time: 388 us -> 53.7 us (0.14)
  blocking collectives: 160 us -> 0 us
  waiting for transfers between devices: 73 us -> 0 us
  starting transfers between devices: 64.1 us -> 0 us
  Pallas kernels: 0 us -> 44.1 us
  other arithmetic: 38.1 us -> 0 us
  matrix products: 22 us -> 0 us
  local copies, waits for them, and re-layouts: 27.4 us -> 8.65 us
    psum x4 -> x0, blocking collectives: 160 us -> none  [the longest x1 40.9 us: orthonormalize(): lax.psum(local_gram(first_resid) * dof_weight, ('gx', 'gy', 'gz'))]
    ppermute x30 -> x0, waiting for transfers between devices: 73 us -> none  [the longest x15 40.5 us: padded_2(): lax.ppermute(lax.slice_in_dim(block, 0, width, axis=dim), axis, backward)]
    ppermute x30 -> x0, starting transfers between devices: 64.1 us -> none  [the longest x15 44.5 us: padded_2(): lax.ppermute(lax.slice_in_dim(block, block.shape[dim] - width, None, axis...]
    pallas_call x0 -> x1, Pallas kernels: none -> 44.1 us  [shards(): pl.pallas_call(functools.partial(kernel, sizes), out_shape=(jax.ShapeDtyp...]
    another operation x52 -> x0, other arithmetic: 23.5 us -> none  [the longest x10 6.42 us: apply_inverse(): jax.scipy.linalg.solve_triangular(lower_factor, identity_block, lower=True)]
    dot_general x36 -> x0, matrix products: 21.1 us -> none  [the longest x4 5.97 us: orthonormalize(): factor = jnp.dot(first_lower, second_lower, precision=highest).T]
    concatenate x11 -> x0, other arithmetic: 12.1 us -> none  [the longest x10 12.1 us: padded_2(): block = jnp.concatenate([low, block, high], axis=dim)]
    ppermute x4 -> x0, local copies, waits for them, and re-layouts: 10.3 us -> none  [the longest x2 5.22 us: padded_2(): lax.ppermute(lax.slice_in_dim(block, 0, width, axis=dim), axis, backward)]
  transfers between devices with their start and end apart: 30 -> 0, of which waited for: 20 -> 0; matrix products, arithmetic and copies ran while one was open for 5% -> 0% of each run, Pallas kernels for 0% -> 0%
where the time goes in v1:
time: 53.7 us; the launch traced here: 53.4 us
  Pallas kernels  44.1 us (82%)
  local copies, waits for them, and re-layouts  8.65 us (16%)
  between operations  0.65 us (1%)
    pallas_call x1, Pallas kernels, shards(): pl.pallas_call(functools.partial(kernel, sizes), out_shape=(jax.ShapeDtyp...  44.1 us
    unnamed x15, local copies, waits for them, and re-layouts  7.86 us

profile of v1, /device:TPU:0, one launch (start us, length us, event | category | flops | bytes accessed | tf_op | source)
XLA Modules:
  0.0 53.4 jit_solution(7705128775327703865)
XLA Ops:
  0.6 0.8 %copy.11.now_ref = bf16[128,8]{1,0:T(8,128)(2,1)S(1)} copy(bf16[128,8]{0,1:T(8,128)(2,1)} %param.8) | data formatting | bytes 4096 | tf_op args[1]
  1.4 0.8 %copy.12.prev_ref = bf16[128,8]{1,0:T(8,128)(2,1)S(1)} copy(bf16[128,8]{0,1:T(8,128)(2,1)} %param.9) | data formatting | bytes 4096 | tf_op args[2]
  2.2 0.0 copy-start
  2.2 1.4 %copy-done = bf16[2,3,8,128,128]{4,3,2,1,0:T(8,128)(2,1)S(1)} copy-done((bf16[2,3,8,128,128]{4,3,2,1,0:T(8,128)(2,1)S(1)}, bf16[2,3,8,128,128]{4,3,2,1,0:T(8,128)(2,1)}, u32[]{:S(2)}) %copy-start) | copy-done | bytes 1572888
  3.6 0.0 copy-start.1
  3.6 0.8 %copy-done.1 = s32[8,2,8,128]{3,2,1,0:T(8,128)S(1)} copy-done((s32[8,2,8,128]{3,2,1,0:T(8,128)S(1)}, s32[8,2,8,128]{3,2,1,0:T(8,128)}, u32[]{:S(2)}) %copy-start.1) | copy-done | bytes 65560
  4.5 0.0 copy-start.2
  4.5 0.7 %copy-done.2 = s32[2,8,128]{2,1,0:T(8,128)S(1)} copy-done((s32[2,8,128]{2,1,0:T(8,128)S(1)}, s32[2,8,128]{2,1,0:T(8,128)}, u32[]{:S(2)}) %copy-start.2) | copy-done | bytes 8216
  5.2 0.0 copy-start.3
  5.2 0.7 %copy-done.3 = f32[3,4]{1,0:T(4,128)S(1)} copy-done((f32[3,4]{1,0:T(4,128)S(1)}, f32[3,4]{1,0:T(4,128)}, u32[]{:S(2)}) %copy-start.3) | copy-done | bytes 72
  5.9 0.0 copy-start.4
  5.9 0.7 %copy-done.4 = f32[3,8]{1,0:T(4,128)S(1)} copy-done((f32[3,8]{1,0:T(4,128)S(1)}, f32[3,8]{1,0:T(4,128)}, u32[]{:S(2)}) %copy-start.4) | copy-done | bytes 120
  6.5 44.1 %shard_map.102 = (f32[3,8,2,8,128]{4,3,2,1,0:T(8,128)S(1)}, f32[3,8,2,8,128]{4,3,2,1,0:T(8,128)S(1)}, f32[4,2,128,8]{3,2,1,0:T(8,128)S(1)}, f32[4,8,8]{2,1,0:T(8,128)S(1)}) custom-call(bf16[2,3,8,128,128]{4,3,2,1,0:T(8,128)(2,1)S(1)} %copy-done, bf16[128,8]{1,0:T(8,128)(2,1)S(1)} %copy.11.now_ref, bf16[128,8]{1,0:T(8,128)(2,1)S(1)} %copy.12.prev_ref, ...), custom_call_target="tpu_custom_call" | custom-call | flops 1000000000 | bytes 3000000 | tf_op jit(solution)/shard_map/pallas_call | solution.py:354
  50.7 0.8 %copy.13 = f32[4,2,128,8]{2,3,1,0:T(8,128)} copy(f32[4,2,128,8]{3,2,1,0:T(8,128)S(1)} %get-tuple-element.6) | data formatting | bytes 65536 | tf_op jit(solution)/shard_map/pallas_call | solution.py:354
  51.4 0.7 %copy.17 = f32[3,8,2,8,128]{4,3,2,1,0:T(8,128)} copy(f32[3,8,2,8,128]{4,3,2,1,0:T(8,128)S(1)} %get-tuple-element.12) | data formatting | bytes 393216
  52.1 0.7 %copy.18 = f32[3,8,2,8,128]{4,3,2,1,0:T(8,128)} copy(f32[3,8,2,8,128]{4,3,2,1,0:T(8,128)S(1)} %get-tuple-element.13) | data formatting | bytes 393216
  52.8 0.6 %copy.19 = f32[4,8,8]{2,1,0:T(8,128)} copy(f32[4,8,8]{2,1,0:T(8,128)S(1)} %get-tuple-element.15) | data formatting | bytes 2048
Async XLA Ops:
  2.2 1.4 %copy-start = (bf16[2,3,8,128,128]{4,3,2,1,0:T(8,128)(2,1)S(1)}, bf16[2,3,8,128,128]{4,3,2,1,0:T(8,128)(2,1)}, u32[]{:S(2)}) copy-start(bf16[2,3,8,128,128]{4,3,2,1,0:T(8,128)(2,1)} %basis_ref.1) | copy-start | bytes 4718596
  3.6 0.8 %copy-start.1 = (s32[8,2,8,128]{3,2,1,0:T(8,128)S(1)}, s32[8,2,8,128]{3,2,1,0:T(8,128)}, u32[]{:S(2)}) copy-start(s32[8,2,8,128]{3,2,1,0:T(8,128)} %mask_ref.1) | copy-start | bytes 196612
  4.5 0.7 %copy-start.2 = (s32[2,8,128]{2,1,0:T(8,128)S(1)}, s32[2,8,128]{2,1,0:T(8,128)}, u32[]{:S(2)}) copy-start(s32[2,8,128]{2,1,0:T(8,128)} %ids_ref.1) | copy-start | bytes 24580
  5.2 0.7 %copy-start.3 = (f32[3,4]{1,0:T(4,128)S(1)}, f32[3,4]{1,0:T(4,128)}, u32[]{:S(2)}) copy-start(f32[3,4]{1,0:T(4,128)} %moduli_ref.1) | copy-start | bytes 148
  5.9 0.7 %copy-start.4 = (f32[3,8]{1,0:T(4,128)S(1)}, f32[3,8]{1,0:T(4,128)}, u32[]{:S(2)}) copy-start(f32[3,8]{1,0:T(4,128)} %drive_ref.1) | copy-start | bytes 292

commit v2 on v1

v2 whole, which is shorter than its diff:
```python
import functools
import jax
import jax.numpy as jnp
from jax import lax
from jax.experimental import pallas as pl
from jax.experimental.pallas import tpu as pltpu
from jax.sharding import PartitionSpec as P

STEPS = 4
MESH_IDS = pl.DeviceIdType.MESH
AXES = ("gx", "gy", "gz")
HIGHEST = lax.Precision.HIGHEST
NT = (((1,), (1,)), ((), ()))
NN = (((1,), (0,)), ((), ()))
TN = (((0,), (0,)), ((), ()))

step_squared = 0.1
ramp_steps = 4.0


def dot32(a, b, dims):
    return lax.dot_general(a, b, dims, precision=HIGHEST, preferred_element_type=jnp.float32)


def dot16(a, b, dims):
    return lax.dot_general(a, b, dims, preferred_element_type=jnp.float32)


def small_product(a, b):
    total = a[:, :, 0:1] * b[:, 0:1, :]
    for k in range(1, b.shape[1]):
        total = total + a[:, :, k : k + 1] * b[:, k : k + 1, :]
    return total


def factor(gram):
    s, n, _ = gram.shape
    rows = lax.broadcasted_iota(jnp.int32, (s, n, 128), 1)
    lanes = lax.broadcasted_iota(jnp.int32, (s, n, 128), 2)
    work = jnp.concatenate([gram, jnp.zeros((s, n, 128 - n), jnp.float32)], axis=2)
    work = jnp.where(lanes == rows + n, 1.0, work)
    pivots = jnp.ones((s, n, 128), jnp.float32)
    for k in range(n):
        pivot = work[:, k : k + 1, k : k + 1]
        pivots = jnp.where(rows == k, pivot, pivots)
        if k < n - 1:
            ratio = jnp.where(rows > k, work[:, :, k : k + 1] / pivot, 0.0)
            work = work - ratio * work[:, k : k + 1, :]
    work = work * lax.rsqrt(pivots)
    upper = jnp.where(lanes >= rows, work, 0.0)[:, :, :n]
    return upper, work[:, :, n : 2 * n]


def kernel(sizes, basis_hbm, both_hbm, ids_hbm, moduli_hbm, mask_hbm, drive_hbm,
           disp_out, modes_out, coef_out, rfac_out,
           disp_ref, modes_ref, coef_ref, rfac_ref, out_sem,
           basis_ref, both_ref, ids_ref, moduli_ref, mask_ref, drive_ref, in_sem,
           field_ref, ids_field_ref, hx_ref, hy_ref, hz_ref, zs_ref,
           ix_ref, iy_ref, iz_ref, izs_ref, coup_ref,
           gpart_ref, gy_buf, gx_buf, gz_buf, gslice_ref, gfull_ref,
           early_a, early_b, late_a, late_b, early_out, late_out,
           halo_send, halo_recv, g_send, g_recv, s_send, s_recv):
    nx, ny, nz = sizes
    count = dict(zip(AXES, sizes))
    me = {axis: lax.axis_index(axis) for axis in AXES}
    X, C, Y, Z, K = basis_ref.shape
    J = both_ref.shape[0] // 2
    tiles = X * C * Y
    weight = 1.0 / (tiles * Z * nx * ny * nz)

    loads = [pltpu.make_async_copy(src, dst, in_sem.at[i]) for i, (src, dst) in enumerate((
        (ids_hbm, ids_ref), (both_hbm, both_ref), (basis_hbm, basis_ref),
        (moduli_hbm, moduli_ref), (mask_hbm, mask_ref), (drive_hbm, drive_ref)))]
    for load in loads:
        load.start()

    for ref in (hx_ref, hy_ref, hz_ref, ix_ref, iy_ref, iz_ref):
        ref[...] = jnp.zeros_like(ref)

    plane = [(dx, dy) for dx in range(nx) for dy in range(ny) if dx or dy]

    def plane_peer(dx, dy):
        return {"gx": lax.rem(me["gx"] + dx, nx), "gy": lax.rem(me["gy"] + dy, ny)}

    barrier = pltpu.get_barrier_semaphore()
    for dx, dy in plane:
        pl.semaphore_signal(barrier, inc=1, device_id=plane_peer(dx, dy), device_id_type=MESH_IDS)
    for d in range(1, nz):
        pl.semaphore_signal(barrier, inc=1, device_id={"gz": lax.rem(me["gz"] + d, nz)},
                            device_id_type=MESH_IDS)
    pl.semaphore_wait(barrier, nx * ny + nz - 2)

    def halo_copies(slot, src, zsrc, dst_x, dst_y, dst_z):
        plan = []
        faces = {
            "gx": (src.at[X - 1], src.at[0], dst_x),
            "gy": (src.at[:, Y - 1], src.at[:, 0], dst_y),
            "gz": (zsrc.at[1], zsrc.at[0], dst_z),
        }
        for n_axis, axis in enumerate(AXES):
            up, down, dst = faces[axis]
            for side, face in ((0, up), (1, down)):
                target = me[axis] + (1 if side == 0 else -1)
                copy = pltpu.make_async_remote_copy(
                    src_ref=face, dst_ref=dst.at[side],
                    send_sem=halo_send.at[slot, 2 * n_axis + side],
                    recv_sem=halo_recv.at[slot, 2 * n_axis + side],
                    device_id={axis: target}, device_id_type=MESH_IDS)
                has_target = (me[axis] < count[axis] - 1) if side == 0 else (me[axis] > 0)
                has_source = (me[axis] > 0) if side == 0 else (me[axis] < count[axis] - 1)
                plan.append((has_target, has_source, copy))
        return plan

    def send_all(plan):
        for has_target, _, copy in plan:
            @pl.when(has_target)
            def _(copy=copy):
                copy.start()

    def recv_all(plan):
        for _, has_source, copy in plan:
            @pl.when(has_source)
            def _(copy=copy):
                copy.wait_recv()

    def drain(plan):
        for has_target, _, copy in plan:
            @pl.when(has_target)
            def _(copy=copy):
                copy.wait_send()

    def z_faces(value, zdst):
        turned = value.reshape(-1, Z).T
        zdst[0] = turned[0:8]
        zdst[1] = turned[Z - 8 : Z]

    def neighbours(value, hx, hy, hz):
        shape = value.shape
        x_lo = jnp.concatenate([hx[0][None], value[:-1]], axis=0)
        x_hi = jnp.concatenate([value[1:], hx[1][None]], axis=0)
        y_lo = jnp.concatenate([hy[0][:, None], value[:, :-1]], axis=1)
        y_hi = jnp.concatenate([value[:, 1:], hy[1][:, None]], axis=1)
        flat = value.reshape(-1, Z)
        lanes = lax.broadcasted_iota(jnp.int32, flat.shape, 1)
        turned = jnp.concatenate(
            [hz[1], jnp.zeros((Z - 16, flat.shape[0]), jnp.float32), hz[0]], axis=0).T
        z_lo = pltpu.roll(jnp.where(lanes == Z - 1, turned, flat), 1, 1)
        z_hi = pltpu.roll(jnp.where(lanes == 0, turned, flat), Z - 1, 1)
        return ((x_lo, x_hi), (y_lo, y_hi), (z_lo.reshape(shape), z_hi.reshape(shape)))

    def start_all(copies):
        for copy in copies:
            copy.start()
        return copies

    def exchange(axis, src_of, dst, send_sem, recv_sem):
        copies = []
        for d in range(1, count[axis]):
            peer = lax.rem(me[axis] + d, count[axis])
            copies.append(pltpu.make_async_remote_copy(
                src_ref=src_of(peer), dst_ref=dst.at[me[axis]],
                send_sem=send_sem.at[d], recv_sem=recv_sem.at[d],
                device_id={axis: peer}, device_id_type=MESH_IDS))
        return start_all(copies)

    def exchange_plane(src, dst, send_sem, recv_sem):
        copies = []
        for i, (dx, dy) in enumerate(plane):
            copies.append(pltpu.make_async_remote_copy(
                src_ref=src, dst_ref=dst.at[me["gx"] * ny + me["gy"]],
                send_sem=send_sem.at[i], recv_sem=recv_sem.at[i],
                device_id=plane_peer(dx, dy), device_id_type=MESH_IDS))
        return start_all(copies)

    def finish(started):
        for copy in started:
            copy.wait_recv()
            copy.wait_send()

    def total_of(buf):
        total = buf[0]
        for i in range(1, buf.shape[0]):
            total = total + buf[i]
        return total

    loads[0].wait()
    idf = (ids_ref[...] + 1).astype(jnp.float32)
    idf = jnp.broadcast_to(idf[:, :, None, :], (X, Y, J, Z))
    ids_field_ref[...] = idf
    z_faces(idf, izs_ref)
    ids_plan = halo_copies(STEPS * C, ids_field_ref, izs_ref, ix_ref, iy_ref, iz_ref)
    send_all(ids_plan)

    loads[1].wait()
    loads[2].wait()
    basis = basis_ref[...].reshape(tiles * Z, K)
    start = dot16(both_ref[...], basis, NT)

    def tile_at(x, c, y):
        t = (x * C + c) * Y + y
        return slice(t * Z, (t + 1) * Z)

    def component(flat, c):
        parts = [flat[:, tile_at(x, c, y)] for x in range(X) for y in range(Y)]
        return jnp.stack(parts).reshape(X, Y, J, Z)

    def as_flat(fields):
        return jnp.concatenate(
            [fields[c][x, y] for x in range(X) for c in range(C) for y in range(Y)], axis=1)

    plans = [[halo_copies(s * C + c, field_ref.at[s + 1, c], zs_ref.at[s, c],
                          hx_ref.at[s, c], hy_ref.at[s, c], hz_ref.at[s, c])
              for c in range(C)] for s in range(STEPS)]

    def publish(step, c, value):
        field_ref[step + 1, c] = value
        if step < STEPS:
            z_faces(value, zs_ref.at[step, c])
            send_all(plans[step][c])

    for c in range(C):
        publish(0, c, component(start[:J], c))
        field_ref[0, c] = component(start[J:], c)

    rows = K // ny
    gpart_ref[...] = dot16(basis, basis, TN).reshape(ny, rows, K)
    gy_buf[me["gy"]] = gpart_ref[me["gy"]]
    g_stage = exchange("gy", lambda p: gpart_ref.at[p], gy_buf, g_send.at[0], g_recv.at[0])

    for load in loads[3:]:
        load.wait()
    recv_all(ids_plan)

    def pick(p, index):
        value = jnp.zeros_like(index)
        for m in range(moduli_ref.shape[1]):
            value = jnp.where(index == float(m + 1), moduli_ref[p, m], value)
        return value

    around = neighbours(idf, ix_ref[...], iy_ref[...], iz_ref[...])
    scale = step_squared * pick(2, idf)
    for p in range(2):
        own = pick(p, idf)
        for a in range(3):
            for side in range(2):
                coup_ref[p, a, side] = 0.5 * scale * (own + pick(p, around[a][side]))
    sub = lax.broadcasted_iota(jnp.int32, (J, Z), 0)
    mask = jnp.stack([mask_ref[:, x, y, :] for x in range(X) for y in range(Y)])
    pushed = scale * mask.astype(jnp.float32).reshape(X, Y, J, Z)
    drives = []
    for c in range(C):
        column = jnp.zeros((J, Z), jnp.float32)
        for j in range(J):
            column = jnp.where(sub == j, drive_ref[c, j], column)
        drives.append(column)

    def advance(step, c):
        recv_all(plans[step][c])
        current = field_ref[step + 1, c]
        around = neighbours(current, hx_ref[step, c], hy_ref[step, c], hz_ref[step, c])
        ramp = min(1.0, (step + 1) / ramp_steps)
        following = 2.0 * current - field_ref[step, c] + pushed * (ramp * drives[c])
        for a in range(3):
            for side in range(2):
                following = following - coup_ref[0 if c == a else 1, a, side] * (current - around[a][side])
        publish(step + 1, c, following)

    def snapshots(first, last, pad):
        parts = [as_flat([field_ref[s + 2, c] for c in range(C)]) for s in range(first, last)]
        parts += [jnp.zeros_like(parts[0])] * pad
        return jnp.concatenate(parts, axis=0).astype(jnp.bfloat16)

    def local_stats(snap, n):
        proj = dot16(snap, basis, NN)[: n * J]
        gram = dot16(snap, snap, NT)
        lanes = lax.broadcasted_iota(jnp.int32, (J, gram.shape[1]), 1)
        side = gram[:J]
        for s in range(1, n):
            side = jnp.where(lanes >= s * J, gram[s * J : (s + 1) * J], side)
        side = jnp.concatenate([side, jnp.zeros((J, K - gram.shape[1]), jnp.float32)], axis=1)
        return jnp.concatenate([proj, side], axis=0) * weight

    def reduce_plane(index, value, out, buf):
        out[0] = value
        buf[me["gx"] * ny + me["gy"]] = value
        return exchange_plane(out.at[0], buf, s_send.at[index, 0], s_recv.at[index, 0])

    def reduce_z(index, started, out, buf, next_buf):
        finish(started)
        value = total_of(buf)
        out[1] = value
        next_buf[me["gz"]] = value
        return exchange("gz", lambda p: out.at[1], next_buf, s_send.at[index, 1], s_recv.at[index, 1])

    for step in range(STEPS):
        for c in range(C):
            advance(step, c)
        if step == 0:
            finish(g_stage)
            gslice_ref[0] = total_of(gy_buf)
            gx_buf[me["gx"]] = gslice_ref[0]
            g_stage = exchange("gx", lambda p: gslice_ref.at[0], gx_buf, g_send.at[1], g_recv.at[1])
        if step == 1:
            finish(g_stage)
            gslice_ref[1] = total_of(gx_buf)
            gz_buf[me["gz"]] = gslice_ref[1]
            g_stage = exchange("gz", lambda p: gslice_ref.at[1], gz_buf, g_send.at[2], g_recv.at[2])
        if step == 2:
            early = reduce_plane(0, local_stats(snapshots(0, 3, 1), 3), early_out, early_a)
            finish(g_stage)
            gslice_ref[2] = total_of(gz_buf) * weight
            gfull_ref[me["gy"]] = gslice_ref[2]
            g_stage = exchange("gy", lambda p: gslice_ref.at[2], gfull_ref, g_send.at[3], g_recv.at[3])

    snap = snapshots(STEPS - 1, STEPS, 1)
    late = reduce_plane(1, local_stats(snap, 1), late_out, late_a)
    early = reduce_z(0, early, early_out, early_a, early_b)
    for x in range(X):
        for c in range(C):
            for y in range(Y):
                disp_ref[c, :, x, y, :] = field_ref[STEPS + 1, c, x, y]
    stores = [pltpu.make_async_copy(src, dst, out_sem.at[i]) for i, (src, dst) in enumerate((
        (disp_ref, disp_out), (modes_ref, modes_out), (coef_ref, coef_out), (rfac_ref, rfac_out)))]
    stores[0].start()
    finish(g_stage)
    gram_basis = gfull_ref[...].reshape(K, K)
    late = reduce_z(1, late, late_out, late_a, late_b)
    finish(early)
    first = total_of(early_b)
    finish(late)
    second = total_of(late_b)

    head = (STEPS - 1) * J
    coef1 = jnp.concatenate([first[:head], second[:J]], axis=0)
    coef1_b = coef1.astype(jnp.bfloat16).astype(jnp.float32)

    def blocks(full):
        return jnp.stack([full[J * s : J * s + J, J * s : J * s + J] for s in range(STEPS)])

    snap_gram = jnp.stack(
        [first[head:, J * s : J * s + J] for s in range(STEPS - 1)] + [second[J:, :J]])
    left = coef1 - dot32(coef1_b, gram_basis, NN)
    gram1 = snap_gram - blocks(dot32(coef1_b, left, NT) + dot32(coef1, coef1_b, NT))
    upper1, inverse1 = factor(gram1)
    coef2 = small_product(inverse1, left.reshape(STEPS, J, K)).reshape(STEPS * J, K)
    coef2_b = coef2.astype(jnp.bfloat16).astype(jnp.float32)
    left2 = coef2 - dot32(coef2_b, gram_basis, NN)
    eye = (lax.broadcasted_iota(jnp.int32, (STEPS, J, J), 1)
           == lax.broadcasted_iota(jnp.int32, (STEPS, J, J), 2)).astype(jnp.float32)
    gram2 = eye - blocks(dot32(coef2_b, left2, NT) + dot32(coef2, coef2_b, NT))
    upper2, inverse2 = factor(gram2)
    rfac_ref[...] = small_product(upper2, upper1)
    for s in range(STEPS):
        coef_ref[s, 0] = coef1[J * s : J * s + J]
        coef_ref[s, 1] = coef2[J * s : J * s + J]

    stores[2].start()
    stores[3].start()

    inv1, inv2 = inverse1[STEPS - 1 :], inverse2[STEPS - 1 :]
    tail = slice(J * (STEPS - 1), J * STEPS)
    mix = small_product(inv1, coef1_b[tail][None]) + coef2_b[tail][None]
    mix = small_product(inv2, mix)[0]
    mix_hi = mix.astype(jnp.bfloat16).astype(jnp.float32)
    parts = jnp.concatenate([mix_hi, mix - mix_hi], axis=0).astype(jnp.bfloat16)
    spread = dot16(parts, basis, NT)
    rounded = snap[:J].astype(jnp.float32)
    modes = small_product(small_product(inv2, inv1), rounded[None])[0]
    modes = modes - (spread[:J] + spread[J:])
    for x in range(X):
        for c in range(C):
            for y in range(Y):
                modes_ref[c, :, x, y, :] = modes[:, tile_at(x, c, y)]

    stores[1].start()
    drain(ids_plan)
    for plan in plans:
        for part in plan:
            drain(part)
    for store in stores:
        store.wait()


def write_out(*refs):
    count = (len(refs) - 1) // 2
    copies = [pltpu.make_async_copy(refs[i], refs[count + i], refs[-1].at[i]) for i in range(count)]
    for copy in copies:
        copy.start()
    for copy in copies:
        copy.wait()


def shards(sizes, basis, modal_now, modal_prev, material_ids, moduli, drive_mask, drive):
    nx, ny, nz = sizes
    X, C, Y, Z, K = basis.shape
    J = modal_now.shape[1]
    f32 = jnp.float32
    hbm = pl.BlockSpec(memory_space=pltpu.HBM)
    rows = K // ny
    most = max(nx * ny, nz)
    both = jnp.concatenate([modal_now.T, modal_prev.T], axis=0)
    shapes = (
        jax.ShapeDtypeStruct((C, J, X, Y, Z), f32),
        jax.ShapeDtypeStruct((C, J, X, Y, Z), f32),
        jax.ShapeDtypeStruct((STEPS, 2, J, K), f32),
        jax.ShapeDtypeStruct((STEPS, J, J), f32),
    )
    results = pl.pallas_call(
        functools.partial(kernel, sizes),
        out_shape=shapes,
        in_specs=[hbm] * 6,
        out_specs=(hbm,) * 4,
        scratch_shapes=[pltpu.VMEM(shape.shape, f32) for shape in shapes] + [
            pltpu.SemaphoreType.DMA((4,)),
            pltpu.VMEM(basis.shape, basis.dtype),
            pltpu.VMEM(both.shape, both.dtype),
            pltpu.VMEM(material_ids.shape, material_ids.dtype),
            pltpu.SMEM(moduli.shape, f32),
            pltpu.VMEM(drive_mask.shape, drive_mask.dtype),
            pltpu.SMEM(drive.shape, f32),
            pltpu.SemaphoreType.DMA((6,)),
            pltpu.VMEM((STEPS + 2, C, X, Y, J, Z), f32),
            pltpu.VMEM((X, Y, J, Z), f32),
            pltpu.VMEM((STEPS, C, 2, Y, J, Z), f32),
            pltpu.VMEM((STEPS, C, 2, X, J, Z), f32),
            pltpu.VMEM((STEPS, C, 2, 8, X * Y * J), f32),
            pltpu.VMEM((STEPS, C, 2, 8, X * Y * J), f32),
            pltpu.VMEM((2, Y, J, Z), f32),
            pltpu.VMEM((2, X, J, Z), f32),
            pltpu.VMEM((2, 8, X * Y * J), f32),
            pltpu.VMEM((2, 8, X * Y * J), f32),
            pltpu.VMEM((2, 3, 2, X, Y, J, Z), f32),
            pltpu.VMEM((ny, rows, K), f32),
            pltpu.VMEM((ny, rows, K), f32),
            pltpu.VMEM((nx, rows, K), f32),
            pltpu.VMEM((nz, rows, K), f32),
            pltpu.VMEM((3, rows, K), f32),
            pltpu.VMEM((ny, rows, K), f32),
            pltpu.VMEM((nx * ny, STEPS * J, K), f32),
            pltpu.VMEM((nz, STEPS * J, K), f32),
            pltpu.VMEM((nx * ny, 2 * J, K), f32),
            pltpu.VMEM((nz, 2 * J, K), f32),
            pltpu.VMEM((2, STEPS * J, K), f32),
            pltpu.VMEM((2, 2 * J, K), f32),
            pltpu.SemaphoreType.DMA((STEPS * C + 1, 6)),
            pltpu.SemaphoreType.DMA((STEPS * C + 1, 6)),
            pltpu.SemaphoreType.DMA((4, max(sizes))),
            pltpu.SemaphoreType.DMA((4, max(sizes))),
            pltpu.SemaphoreType.DMA((2, 2, most)),
            pltpu.SemaphoreType.DMA((2, 2, most)),
        ],
        compiler_params=pltpu.CompilerParams(
            collective_id=0, has_side_effects=True, vmem_limit_bytes=66650000),
        cost_estimate=pl.CostEstimate(flops=1000000000, bytes_accessed=3000000, transcendentals=0),
    )(basis, both, material_ids, moduli, drive_mask, drive)
    disp, modes, coefs, factors = pl.pallas_call(
        write_out,
        out_shape=shapes,
        in_specs=[hbm] * 4,
        out_specs=(hbm,) * 4,
        scratch_shapes=[pltpu.SemaphoreType.DMA((4,))],
    )(*results)
    return disp, modes, jnp.swapaxes(coefs, 2, 3), factors


def solution(mesh):
    sizes = tuple(mesh.shape[axis] for axis in AXES)
    in_specs = (
        P("gx", None, "gy", "gz", None),
        P(),
        P(),
        P("gx", "gy", "gz"),
        P(),
        P(None, "gx", "gy", "gz"),
        P(),
    )
    out_specs = (P(None, None, "gx", "gy", "gz"), P(None, None, "gx", "gy", "gz"), P(), P())
    return jax.shard_map(functools.partial(shards, sizes), mesh=mesh, in_specs=in_specs,
                         out_specs=out_specs, check_vma=False)
```

time: 53.7 us -> 57.7 us (1.074)
  Pallas kernels: 44.1 us -> 55.5 us
  local copies, waits for them, and re-layouts: 8.65 us -> 0 us
  other arithmetic: 0 us -> 1.29 us
    pallas_call x1 -> x2, Pallas kernels: 44.1 us -> 55.5 us  [the longest x1 41 us: shards(): pl.pallas_call(functools.partial(kernel, sizes), out_shape=shapes, in_spe...]
    unnamed x15 -> x0, local copies, waits for them, and re-layouts: 7.86 us -> none
    concatenate x0 -> x1, other arithmetic: none -> 1.29 us  [shards(): both = jnp.concatenate([modal_now.T, modal_prev.T], axis=0)]
    pallas_call x1 -> x0, local copies, waits for them, and re-layouts: 0.79 us -> none  [shards(): pl.pallas_call(functools.partial(kernel, sizes), out_shape=(jax.ShapeDtyp...]
where the time goes in v2:
time: 57.7 us; the launch traced here: 57.5 us
  Pallas kernels  55.5 us (96%)
  other arithmetic  1.29 us (2%)
  between operations  0.64 us (1%)
    pallas_call x1, Pallas kernels, shards(): pl.pallas_call(functools.partial(kernel, sizes), out_shape=shapes, in_spe...  41 us
    pallas_call x1, Pallas kernels, shards(): pl.pallas_call(write_out, out_shape=shapes, in_specs=[hbm] * 4, out_specs...  14.5 us
    concatenate x1, other arithmetic, shards(): both = jnp.concatenate([modal_now.T, modal_prev.T], axis=0)  1.29 us

profile of v2, /device:TPU:0, one launch (start us, length us, event | category | flops | bytes accessed | tf_op | source)
XLA Modules:
  0.0 57.5 jit_solution(925744180880311649)
XLA Ops:
  0.6 1.3 %pad_maximum_fusion.both_hbm = bf16[16,128]{1,0:T(8,128)(2,1)} fusion(bf16[8,128]{1,0:T(8,128)(2,1)} %bitcast.3, bf16[8,128]{1,0:T(8,128)(2,1)} %bitcast.4), kind=kLoop, calls=%fused_computation | loop fusion | flops 8192 | bytes 8192 | tf_op jit(solution)/shard_map/concatenate | solution.py:401
  1.9 41.0 %shard_map.102 = (f32[3,8,2,8,128]{4,3,2,1,0:T(8,128)}, f32[3,8,2,8,128]{4,3,2,1,0:T(8,128)}, f32[4,2,8,128]{3,2,1,0:T(8,128)}, f32[4,8,8]{2,1,0:T(8,128)}) custom-call(bf16[2,3,8,128,128]{4,3,2,1,0:T(8,128)(2,1)} %basis_hbm.1, bf16[16,128]{1,0:T(8,128)(2,1)} %pad_maximum_fusion.both_hbm, s32[2,8,128]{2,1,0:T(8,128)} %ids_hbm.1, f32[3,4]{1,0:T(4,128)} %moduli_hbm.1, ...), custom_call_target="tpu_custom_call" | custom-call | flops 1000000000 | bytes 3000000 | tf_op jit(solution)/shard_map/pallas_call | solution.py:408
  42.9 14.5 %shard_map.103 = (f32[3,8,2,8,128]{4,3,2,1,0:T(8,128)}, f32[3,8,2,8,128]{4,3,2,1,0:T(8,128)}, f32[4,2,8,128]{3,2,1,0:T(8,128)}, f32[4,8,8]{2,1,0:T(8,128)}) custom-call(f32[3,8,2,8,128]{4,3,2,1,0:T(8,128)} %get-tuple-element.12.refs_0_, f32[3,8,2,8,128]{4,3,2,1,0:T(8,128)} %get-tuple-element.13.refs_1_, f32[4,2,8,128]{3,2,1,0:T(8,128)} %get-tuple-element.14.refs_2_, ...), custom_call_target="tpu_custom_call" | custom-call | tf_op jit(solution)/shard_map/pallas_call | solution.py:456

commit v3 on v2

--- a/solution.py
+++ b/solution.py
@@ -9,17 +9,12 @@
 STEPS = 4
 MESH_IDS = pl.DeviceIdType.MESH
 AXES = ("gx", "gy", "gz")
-HIGHEST = lax.Precision.HIGHEST
 NT = (((1,), (1,)), ((), ()))
 NN = (((1,), (0,)), ((), ()))
 TN = (((0,), (0,)), ((), ()))
 
 step_squared = 0.1
 ramp_steps = 4.0
-
-
-def dot32(a, b, dims):
-    return lax.dot_general(a, b, dims, precision=HIGHEST, preferred_element_type=jnp.float32)
 
 
 def dot16(a, b, dims):
@@ -39,22 +34,34 @@
     lanes = lax.broadcasted_iota(jnp.int32, (s, n, 128), 2)
     work = jnp.concatenate([gram, jnp.zeros((s, n, 128 - n), jnp.float32)], axis=2)
     work = jnp.where(lanes == rows + n, 1.0, work)
+    columns = [jnp.broadcast_to(gram[:, :, j : j + 1], (s, n, 128)) for j in range(n)]
     pivots = jnp.ones((s, n, 128), jnp.float32)
     for k in range(n):
-        pivot = work[:, k : k + 1, k : k + 1]
+        pivot = columns[k][:, k : k + 1]
         pivots = jnp.where(rows == k, pivot, pivots)
         if k < n - 1:
-            ratio = jnp.where(rows > k, work[:, :, k : k + 1] / pivot, 0.0)
-            work = work - ratio * work[:, k : k + 1, :]
+            ratio = jnp.where(rows > k, columns[k] * (1.0 / pivot), 0.0)
+            work = work - ratio * work[:, k : k + 1]
+            for j in range(k + 1, n):
+                columns[j] = columns[j] - ratio * columns[j][:, k : k + 1]
     work = work * lax.rsqrt(pivots)
     upper = jnp.where(lanes >= rows, work, 0.0)[:, :, :n]
     return upper, work[:, :, n : 2 * n]
 
 
-def kernel(sizes, basis_hbm, both_hbm, ids_hbm, moduli_hbm, mask_hbm, drive_hbm,
+def in_parts(value):
+    parts = []
+    for _ in range(3):
+        part = value.astype(jnp.bfloat16)
+        parts.append(part)
+        value = value - part.astype(jnp.float32)
+    return parts
+
+
+def kernel(sizes, basis_hbm, now_hbm, prev_hbm, ids_hbm, moduli_hbm, mask_hbm, drive_hbm,
            disp_out, modes_out, coef_out, rfac_out,
            disp_ref, modes_ref, coef_ref, rfac_ref, out_sem,
-           basis_ref, both_ref, ids_ref, moduli_ref, mask_ref, drive_ref, in_sem,
+           basis_ref, now_ref, prev_ref, ids_ref, moduli_ref, mask_ref, drive_ref, in_sem,
            field_ref, ids_field_ref, hx_ref, hy_ref, hz_ref, zs_ref,
            ix_ref, iy_ref, iz_ref, izs_ref, coup_ref,
            gpart_ref, gy_buf, gx_buf, gz_buf, gslice_ref, gfull_ref,
@@ -64,12 +71,12 @@
     count = dict(zip(AXES, sizes))
     me = {axis: lax.axis_index(axis) for axis in AXES}
     X, C, Y, Z, K = basis_ref.shape
-    J = both_ref.shape[0] // 2
+    J = now_ref.shape[0]
     tiles = X * C * Y
     weight = 1.0 / (tiles * Z * nx * ny * nz)
 
     loads = [pltpu.make_async_copy(src, dst, in_sem.at[i]) for i, (src, dst) in enumerate((
-        (ids_hbm, ids_ref), (both_hbm, both_ref), (basis_hbm, basis_ref),
+        (ids_hbm, ids_ref), (now_hbm, now_ref), (prev_hbm, prev_ref), (basis_hbm, basis_ref),
         (moduli_hbm, moduli_ref), (mask_hbm, mask_ref), (drive_hbm, drive_ref)))]
     for load in loads:
         load.start()
@@ -191,10 +198,11 @@
     ids_plan = halo_copies(STEPS * C, ids_field_ref, izs_ref, ix_ref, iy_ref, iz_ref)
     send_all(ids_plan)
 
-    loads[1].wait()
-    loads[2].wait()
+    for load in loads[1:4]:
+        load.wait()
     basis = basis_ref[...].reshape(tiles * Z, K)
-    start = dot16(both_ref[...], basis, NT)
+    both = jnp.concatenate([now_ref[...].astype(jnp.float32), prev_ref[...].astype(jnp.float32)], axis=0)
+    start = dot16(both.astype(jnp.bfloat16), basis, NT)
 
     def tile_at(x, c, y):
         t = (x * C + c) * Y + y
@@ -227,7 +235,7 @@
     gy_buf[me["gy"]] = gpart_ref[me["gy"]]
     g_stage = exchange("gy", lambda p: gpart_ref.at[p], gy_buf, g_send.at[0], g_recv.at[0])
 
-    for load in loads[3:]:
+    for load in loads[4:]:
         load.wait()
     recv_all(ids_plan)
 
@@ -323,7 +331,7 @@
         (disp_ref, disp_out), (modes_ref, modes_out), (coef_ref, coef_out), (rfac_ref, rfac_out)))]
     stores[0].start()
     finish(g_stage)
-    gram_basis = gfull_ref[...].reshape(K, K)
+    gram_parts = jnp.concatenate(in_parts(gfull_ref[...].reshape(K, K)), axis=0)
     late = reduce_z(1, late, late_out, late_a, late_b)
     finish(early)
     first = total_of(early_b)
@@ -332,41 +340,41 @@
 
     head = (STEPS - 1) * J
     coef1 = jnp.concatenate([first[:head], second[:J]], axis=0)
-    coef1_b = coef1.astype(jnp.bfloat16).astype(jnp.float32)
+    coef1_b = coef1.astype(jnp.bfloat16)
+    tail = slice(J * (STEPS - 1), J * STEPS)
 
     def blocks(full):
         return jnp.stack([full[J * s : J * s + J, J * s : J * s + J] for s in range(STEPS)])
 
+    def less_gram(coef, rounded):
+        return coef - dot16(jnp.concatenate([rounded] * 3, axis=1), gram_parts, NN)
+
+    def cross(coef, rounded, left):
+        lhs = jnp.concatenate([rounded] * 3 + in_parts(coef), axis=1)
+        rhs = jnp.concatenate(in_parts(left) + [rounded] * 3, axis=1)
+        return blocks(dot16(lhs, rhs, NT))
+
     snap_gram = jnp.stack(
         [first[head:, J * s : J * s + J] for s in range(STEPS - 1)] + [second[J:, :J]])
-    left = coef1 - dot32(coef1_b, gram_basis, NN)
-    gram1 = snap_gram - blocks(dot32(coef1_b, left, NT) + dot32(coef1, coef1_b, NT))
+    left = less_gram(coef1, coef1_b)
+    gram1 = snap_gram - cross(coef1, coef1_b, left)
+    resid = snap[:J].astype(jnp.float32) - dot16(coef1_b[tail], basis, NT)
     upper1, inverse1 = factor(gram1)
     coef2 = small_product(inverse1, left.reshape(STEPS, J, K)).reshape(STEPS * J, K)
-    coef2_b = coef2.astype(jnp.bfloat16).astype(jnp.float32)
-    left2 = coef2 - dot32(coef2_b, gram_basis, NN)
+    coef2_b = coef2.astype(jnp.bfloat16)
+    left2 = less_gram(coef2, coef2_b)
     eye = (lax.broadcasted_iota(jnp.int32, (STEPS, J, J), 1)
            == lax.broadcasted_iota(jnp.int32, (STEPS, J, J), 2)).astype(jnp.float32)
-    gram2 = eye - blocks(dot32(coef2_b, left2, NT) + dot32(coef2, coef2_b, NT))
+    gram2 = eye - cross(coef2, coef2_b, left2)
+    resid2 = small_product(inverse1[STEPS - 1 :], resid[None])[0] - dot16(coef2_b[tail], basis, NT)
     upper2, inverse2 = factor(gram2)
+    modes = small_product(inverse2[STEPS - 1 :], resid2[None])[0]
     rfac_ref[...] = small_product(upper2, upper1)
     for s in range(STEPS):
         coef_ref[s, 0] = coef1[J * s : J * s + J]
         coef_ref[s, 1] = coef2[J * s : J * s + J]
-
     stores[2].start()
     stores[3].start()
-
-    inv1, inv2 = inverse1[STEPS - 1 :], inverse2[STEPS - 1 :]
-    tail = slice(J * (STEPS - 1), J * STEPS)
-    mix = small_product(inv1, coef1_b[tail][None]) + coef2_b[tail][None]
-    mix = small_product(inv2, mix)[0]
-    mix_hi = mix.astype(jnp.bfloat16).astype(jnp.float32)
-    parts = jnp.concatenate([mix_hi, mix - mix_hi], axis=0).astype(jnp.bfloat16)
-    spread = dot16(parts, basis, NT)
-    rounded = snap[:J].astype(jnp.float32)
-    modes = small_product(small_product(inv2, inv1), rounded[None])[0]
-    modes = modes - (spread[:J] + spread[J:])
     for x in range(X):
         for c in range(C):
             for y in range(Y):
@@ -382,12 +390,14 @@
 
 
 def write_out(*refs):
-    count = (len(refs) - 1) // 2
-    copies = [pltpu.make_async_copy(refs[i], refs[count + i], refs[-1].at[i]) for i in range(count)]
-    for copy in copies:
-        copy.start()
-    for copy in copies:
-        copy.wait()
+    count = (len(refs) - 2) // 3
+    sources, results, staged = (refs[count * i : count * (i + 1)] for i in range(3))
+    for ends, sem in ((zip(sources, staged), refs[-2]), (zip(staged, results), refs[-1])):
+        copies = [pltpu.make_async_copy(src, dst, sem.at[i]) for i, (src, dst) in enumerate(ends)]
+        for copy in copies:
+            copy.start()
+        for copy in copies:
+            copy.wait()
 
 
 def shards(sizes, basis, modal_now, modal_prev, material_ids, moduli, drive_mask, drive):
@@ -398,7 +408,7 @@
     hbm = pl.BlockSpec(memory_space=pltpu.HBM)
     rows = K // ny
     most = max(nx * ny, nz)
-    both = jnp.concatenate([modal_now.T, modal_prev.T], axis=0)
+    now, prev = modal_now.T, modal_prev.T
     shapes = (
         jax.ShapeDtypeStruct((C, J, X, Y, Z), f32),
         jax.ShapeDtypeStruct((C, J, X, Y, Z), f32),
@@ -408,17 +418,18 @@
     results = pl.pallas_call(
         functools.partial(kernel, sizes),
         out_shape=shapes,
-        in_specs=[hbm] * 6,
+        in_specs=[hbm] * 7,
         out_specs=(hbm,) * 4,
         scratch_shapes=[pltpu.VMEM(shape.shape, f32) for shape in shapes] + [
             pltpu.SemaphoreType.DMA((4,)),
             pltpu.VMEM(basis.shape, basis.dtype),
-            pltpu.VMEM(both.shape, both.dtype),
+            pltpu.VMEM(now.shape, now.dtype),
+            pltpu.VMEM(prev.shape, prev.dtype),
             pltpu.VMEM(material_ids.shape, material_ids.dtype),
             pltpu.SMEM(moduli.shape, f32),
             pltpu.VMEM(drive_mask.shape, drive_mask.dtype),
             pltpu.SMEM(drive.shape, f32),
-            pltpu.SemaphoreType.DMA((6,)),
+            pltpu.SemaphoreType.DMA((7,)),
             pltpu.VMEM((STEPS + 2, C, X, Y, J, Z), f32),
             pltpu.VMEM((X, Y, J, Z), f32),
             pltpu.VMEM((STEPS, C, 2, Y, J, Z), f32),
@@ -452,13 +463,15 @@
         compiler_params=pltpu.CompilerParams(
             collective_id=0, has_side_effects=True, vmem_limit_bytes=66650000),
         cost_estimate=pl.CostEstimate(flops=1000000000, bytes_accessed=3000000, transcendentals=0),
-    )(basis, both, material_ids, moduli, drive_mask, drive)
+    )(basis, now, prev, material_ids, moduli, drive_mask, drive)
     disp, modes, coefs, factors = pl.pallas_call(
         write_out,
         out_shape=shapes,
         in_specs=[hbm] * 4,
         out_specs=(hbm,) * 4,
-        scratch_shapes=[pltpu.SemaphoreType.DMA((4,))],
+        scratch_shapes=[pltpu.VMEM(shape.shape, f32) for shape in shapes] + [
+            pltpu.SemaphoreType.DMA((4,)), pltpu.SemaphoreType.DMA((4,))],
+        compiler_params=pltpu.CompilerParams(vmem_limit_bytes=66650000),
     )(*results)
     return disp, modes, jnp.swapaxes(coefs, 2, 3), factors
 

time: 57.7 us -> 42.4 us (0.73)
  Pallas kernels: 55.5 us -> 41.6 us
  other arithmetic: 1.29 us -> 0 us
    pallas_call x1, Pallas kernels: 14.5 us -> 1.84 us  [shards(): pl.pallas_call(write_out, out_shape=shapes, in_specs=[hbm] * 4, out_specs...]
    concatenate x1 -> x0, other arithmetic: 1.29 us -> none  [shards(): both = jnp.concatenate([modal_now.T, modal_prev.T], axis=0)]
    pallas_call x1, Pallas kernels: 41 us -> 39.7 us  [shards(): pl.pallas_call(functools.partial(kernel, sizes), out_shape=shapes, in_spe...]
where the time goes in v3:
time: 42.4 us; the launch traced here: 42.2 us
  Pallas kernels  41.6 us (98%)
  between operations  0.64 us (2%)
    pallas_call x1, Pallas kernels, shards(): pl.pallas_call(functools.partial(kernel, sizes), out_shape=shapes, in_spe...  39.7 us
    pallas_call x1, Pallas kernels, shards(): pl.pallas_call(write_out, out_shape=shapes, in_specs=[hbm] * 4, out_specs...  1.84 us

profile of v3, /device:TPU:0, one launch (start us, length us, event | category | flops | bytes accessed | tf_op | source)
XLA Modules:
  0.0 42.2 jit_solution(9963368919276133075)
XLA Ops:
  0.6 39.7 %shard_map.102 = (f32[3,8,2,8,128]{4,3,2,1,0:T(8,128)}, f32[3,8,2,8,128]{4,3,2,1,0:T(8,128)}, f32[4,2,8,128]{3,2,1,0:T(8,128)}, f32[4,8,8]{2,1,0:T(8,128)}) custom-call(bf16[2,3,8,128,128]{4,3,2,1,0:T(8,128)(2,1)} %basis_hbm.1, bf16[8,128]{1,0:T(8,128)(2,1)} %bitcast.4, bf16[8,128]{1,0:T(8,128)(2,1)} %bitcast.5, s32[2,8,128]{2,1,0:T(8,128)} %ids_hbm.1, ...), custom_call_target="tpu_custom_call" | custom-call | flops 1000000000 | bytes 3000000 | tf_op jit(solution)/shard_map/pallas_call | solution.py:418
  40.4 1.8 %shard_map.103 = (f32[3,8,2,8,128]{4,3,2,1,0:T(8,128)}, f32[3,8,2,8,128]{4,3,2,1,0:T(8,128)}, f32[4,2,8,128]{3,2,1,0:T(8,128)}, f32[4,8,8]{2,1,0:T(8,128)}) custom-call(f32[3,8,2,8,128]{4,3,2,1,0:T(8,128)} %get-tuple-element.12.refs_0_, f32[3,8,2,8,128]{4,3,2,1,0:T(8,128)} %get-tuple-element.13.refs_1_, f32[4,2,8,128]{3,2,1,0:T(8,128)} %get-tuple-element.14.refs_2_, ...), custom_call_target="tpu_custom_call" | custom-call | tf_op jit(solution)/shard_map/pallas_call | solution.py:467

commit v4 on v3

--- a/solution.py
+++ b/solution.py
@@ -62,7 +62,7 @@
            disp_out, modes_out, coef_out, rfac_out,
            disp_ref, modes_ref, coef_ref, rfac_ref, out_sem,
            basis_ref, now_ref, prev_ref, ids_ref, moduli_ref, mask_ref, drive_ref, in_sem,
-           field_ref, ids_field_ref, hx_ref, hy_ref, hz_ref, zs_ref,
+           field_ref, ids_field_ref, ids_small_ref, hx_ref, hy_ref, hz_ref, zs_ref,
            ix_ref, iy_ref, iz_ref, izs_ref, coup_ref,
            gpart_ref, gy_buf, gx_buf, gz_buf, gslice_ref, gfull_ref,
            early_a, early_b, late_a, late_b, early_out, late_out,
@@ -76,9 +76,11 @@
     weight = 1.0 / (tiles * Z * nx * ny * nz)
 
     loads = [pltpu.make_async_copy(src, dst, in_sem.at[i]) for i, (src, dst) in enumerate((
-        (ids_hbm, ids_ref), (now_hbm, now_ref), (prev_hbm, prev_ref), (basis_hbm, basis_ref),
+        (ids_hbm, ids_ref), (now_hbm, now_ref), (prev_hbm, prev_ref),
         (moduli_hbm, moduli_ref), (mask_hbm, mask_ref), (drive_hbm, drive_ref)))]
-    for load in loads:
+    chunks = [pltpu.make_async_copy(basis_hbm.at[:, c], basis_ref.at[:, c], in_sem.at[len(loads) + c])
+              for c in range(C)]
+    for load in loads[:3] + chunks + loads[3:]:
         load.start()
 
     for ref in (hx_ref, hy_ref, hz_ref, ix_ref, iy_ref, iz_ref):
@@ -97,10 +99,10 @@
                             device_id_type=MESH_IDS)
     pl.semaphore_wait(barrier, nx * ny + nz - 2)
 
-    def halo_copies(slot, src, zsrc, dst_x, dst_y, dst_z):
+    def halo_copies(slot, xsrc, src, zsrc, dst_x, dst_y, dst_z):
         plan = []
         faces = {
-            "gx": (src.at[X - 1], src.at[0], dst_x),
+            "gx": (xsrc.at[X - 1], xsrc.at[0], dst_x),
             "gy": (src.at[:, Y - 1], src.at[:, 0], dst_y),
             "gz": (zsrc.at[1], zsrc.at[0], dst_z),
         }
@@ -130,11 +132,12 @@
             def _(copy=copy):
                 copy.wait_recv()
 
-    def drain(plan):
-        for has_target, _, copy in plan:
-            @pl.when(has_target)
-            def _(copy=copy):
-                copy.wait_send()
+    def drain(all_plans):
+        for n_copy in range(len(all_plans[0])):
+            @pl.when(all_plans[0][n_copy][0])
+            def _(n_copy=n_copy):
+                for plan in all_plans:
+                    plan[n_copy][2].wait_send()
 
     def z_faces(value, zdst):
         turned = value.reshape(-1, Z).T
@@ -192,31 +195,34 @@
 
     loads[0].wait()
     idf = (ids_ref[...] + 1).astype(jnp.float32)
+    ids_small_ref[...] = idf
     idf = jnp.broadcast_to(idf[:, :, None, :], (X, Y, J, Z))
     ids_field_ref[...] = idf
     z_faces(idf, izs_ref)
-    ids_plan = halo_copies(STEPS * C, ids_field_ref, izs_ref, ix_ref, iy_ref, iz_ref)
+    ids_plan = halo_copies(STEPS * C, ids_small_ref, ids_field_ref, izs_ref, ix_ref, iy_ref, iz_ref)
     send_all(ids_plan)
 
-    for load in loads[1:4]:
+    for load in loads[1:3]:
         load.wait()
-    basis = basis_ref[...].reshape(tiles * Z, K)
     both = jnp.concatenate([now_ref[...].astype(jnp.float32), prev_ref[...].astype(jnp.float32)], axis=0)
-    start = dot16(both.astype(jnp.bfloat16), basis, NT)
+    both = both.astype(jnp.bfloat16)
 
     def tile_at(x, c, y):
         t = (x * C + c) * Y + y
         return slice(t * Z, (t + 1) * Z)
 
-    def component(flat, c):
-        parts = [flat[:, tile_at(x, c, y)] for x in range(X) for y in range(Y)]
+    def component(flat):
+        parts = [flat[:, t * Z : (t + 1) * Z] for t in range(X * Y)]
         return jnp.stack(parts).reshape(X, Y, J, Z)
+
+    def part_flat(field):
+        return jnp.concatenate([field[x, y] for x in range(X) for y in range(Y)], axis=1)
 
     def as_flat(fields):
         return jnp.concatenate(
             [fields[c][x, y] for x in range(X) for c in range(C) for y in range(Y)], axis=1)
 
-    plans = [[halo_copies(s * C + c, field_ref.at[s + 1, c], zs_ref.at[s, c],
+    plans = [[halo_copies(s * C + c, field_ref.at[s + 1, c], field_ref.at[s + 1, c], zs_ref.at[s, c],
                           hx_ref.at[s, c], hy_ref.at[s, c], hz_ref.at[s, c])
               for c in range(C)] for s in range(STEPS)]
 
@@ -227,15 +233,18 @@
             send_all(plans[step][c])
 
     for c in range(C):
-        publish(0, c, component(start[:J], c))
-        field_ref[0, c] = component(start[J:], c)
+        chunks[c].wait()
+        start = dot16(both, basis_ref[:, c].reshape(X * Y * Z, K), NT)
+        publish(0, c, component(start[:J]))
+        field_ref[0, c] = component(start[J:])
+    basis = basis_ref[...].reshape(tiles * Z, K)
 
     rows = K // ny
     gpart_ref[...] = dot16(basis, basis, TN).reshape(ny, rows, K)
     gy_buf[me["gy"]] = gpart_ref[me["gy"]]
     g_stage = exchange("gy", lambda p: gpart_ref.at[p], gy_buf, g_send.at[0], g_recv.at[0])
 
-    for load in loads[4:]:
+    for load in loads[3:]:
         load.wait()
     recv_all(ids_plan)
 
@@ -245,7 +254,8 @@
             value = jnp.where(index == float(m + 1), moduli_ref[p, m], value)
         return value
 
-    around = neighbours(idf, ix_ref[...], iy_ref[...], iz_ref[...])
+    side_x = jnp.broadcast_to(ix_ref[...][:, :, None, :], (2, Y, J, Z))
+    around = neighbours(idf, side_x, iy_ref[...], iz_ref[...])
     scale = step_squared * pick(2, idf)
     for p in range(2):
         own = pick(p, idf)
@@ -279,8 +289,10 @@
         return jnp.concatenate(parts, axis=0).astype(jnp.bfloat16)
 
     def local_stats(snap, n):
-        proj = dot16(snap, basis, NN)[: n * J]
-        gram = dot16(snap, snap, NT)
+        return pack_stats(dot16(snap, basis, NN), dot16(snap, snap, NT), n)
+
+    def pack_stats(proj, gram, n):
+        proj = proj[: n * J]
         lanes = lax.broadcasted_iota(jnp.int32, (J, gram.shape[1]), 1)
         side = gram[:J]
         for s in range(1, n):
@@ -300,9 +312,15 @@
         next_buf[me["gz"]] = value
         return exchange("gz", lambda p: out.at[1], next_buf, s_send.at[index, 1], s_recv.at[index, 1])
 
+    proj = gram = 0.0
     for step in range(STEPS):
         for c in range(C):
             advance(step, c)
+            if step == STEPS - 1:
+                part = part_flat(field_ref[STEPS + 1, c])
+                part = jnp.concatenate([part, jnp.zeros_like(part)], axis=0).astype(jnp.bfloat16)
+                proj = proj + dot16(part, basis_ref[:, c].reshape(X * Y * Z, K), NN)
+                gram = gram + dot16(part, part, NT)
         if step == 0:
             finish(g_stage)
             gslice_ref[0] = total_of(gy_buf)
@@ -320,8 +338,7 @@
             gfull_ref[me["gy"]] = gslice_ref[2]
             g_stage = exchange("gy", lambda p: gslice_ref.at[2], gfull_ref, g_send.at[3], g_recv.at[3])
 
-    snap = snapshots(STEPS - 1, STEPS, 1)
-    late = reduce_plane(1, local_stats(snap, 1), late_out, late_a)
+    late = reduce_plane(1, pack_stats(proj, gram, 1), late_out, late_a)
     early = reduce_z(0, early, early_out, early_a, early_b)
     for x in range(X):
         for c in range(C):
@@ -330,11 +347,13 @@
     stores = [pltpu.make_async_copy(src, dst, out_sem.at[i]) for i, (src, dst) in enumerate((
         (disp_ref, disp_out), (modes_ref, modes_out), (coef_ref, coef_out), (rfac_ref, rfac_out)))]
     stores[0].start()
+    drain([ids_plan] + [part for plan in plans for part in plan])
     finish(g_stage)
     gram_parts = jnp.concatenate(in_parts(gfull_ref[...].reshape(K, K)), axis=0)
     late = reduce_z(1, late, late_out, late_a, late_b)
     finish(early)
     first = total_of(early_b)
+    snap = as_flat([field_ref[STEPS + 1, c] for c in range(C)]).astype(jnp.bfloat16)
     finish(late)
     second = total_of(late_b)
 
@@ -358,7 +377,7 @@
         [first[head:, J * s : J * s + J] for s in range(STEPS - 1)] + [second[J:, :J]])
     left = less_gram(coef1, coef1_b)
     gram1 = snap_gram - cross(coef1, coef1_b, left)
-    resid = snap[:J].astype(jnp.float32) - dot16(coef1_b[tail], basis, NT)
+    resid = snap.astype(jnp.float32) - dot16(coef1_b[tail], basis, NT)
     upper1, inverse1 = factor(gram1)
     coef2 = small_product(inverse1, left.reshape(STEPS, J, K)).reshape(STEPS * J, K)
     coef2_b = coef2.astype(jnp.bfloat16)
@@ -381,10 +400,6 @@
                 modes_ref[c, :, x, y, :] = modes[:, tile_at(x, c, y)]
 
     stores[1].start()
-    drain(ids_plan)
-    for plan in plans:
-        for part in plan:
-            drain(part)
     for store in stores:
         store.wait()
 
@@ -429,14 +444,15 @@
             pltpu.SMEM(moduli.shape, f32),
             pltpu.VMEM(drive_mask.shape, drive_mask.dtype),
             pltpu.SMEM(drive.shape, f32),
-            pltpu.SemaphoreType.DMA((7,)),
+            pltpu.SemaphoreType.DMA((6 + C,)),
             pltpu.VMEM((STEPS + 2, C, X, Y, J, Z), f32),
             pltpu.VMEM((X, Y, J, Z), f32),
+            pltpu.VMEM((X, Y, Z), f32),
             pltpu.VMEM((STEPS, C, 2, Y, J, Z), f32),
             pltpu.VMEM((STEPS, C, 2, X, J, Z), f32),
             pltpu.VMEM((STEPS, C, 2, 8, X * Y * J), f32),
             pltpu.VMEM((STEPS, C, 2, 8, X * Y * J), f32),
-            pltpu.VMEM((2, Y, J, Z), f32),
+            pltpu.VMEM((2, Y, Z), f32),
             pltpu.VMEM((2, X, J, Z), f32),
             pltpu.VMEM((2, 8, X * Y * J), f32),
             pltpu.VMEM((2, 8, X * Y * J), f32),

time: 42.4 us -> 41.3 us (0.974)
  Pallas kernels: 41.6 us -> 40.5 us
    pallas_call x1, Pallas kernels: 39.7 us -> 38.7 us  [shards(): pl.pallas_call(functools.partial(kernel, sizes), out_shape=shapes, in_spe...]
where the time goes in v4:
time: 41.3 us; the launch traced here: 41.1 us
  Pallas kernels  40.5 us (98%)
  between operations  0.64 us (2%)
    pallas_call x1, Pallas kernels, shards(): pl.pallas_call(functools.partial(kernel, sizes), out_shape=shapes, in_spe...  38.7 us
    pallas_call x1, Pallas kernels, shards(): pl.pallas_call(write_out, out_shape=shapes, in_specs=[hbm] * 4, out_specs...  1.84 us

profile of v4, /device:TPU:0, one launch (start us, length us, event | category | flops | bytes accessed | tf_op | source)
XLA Modules:
  0.0 41.1 jit_solution(1713013105822274562)
XLA Ops:
  0.6 38.7 %shard_map.102 = (f32[3,8,2,8,128]{4,3,2,1,0:T(8,128)}, f32[3,8,2,8,128]{4,3,2,1,0:T(8,128)}, f32[4,2,8,128]{3,2,1,0:T(8,128)}, f32[4,8,8]{2,1,0:T(8,128)}) custom-call(bf16[2,3,8,128,128]{4,3,2,1,0:T(8,128)(2,1)} %basis_hbm.1, bf16[8,128]{1,0:T(8,128)(2,1)} %bitcast.4, bf16[8,128]{1,0:T(8,128)(2,1)} %bitcast.5, s32[2,8,128]{2,1,0:T(8,128)} %ids_hbm.1, ...), custom_call_target="tpu_custom_call" | custom-call | flops 1000000000 | bytes 3000000 | tf_op jit(solution)/shard_map/pallas_call | solution.py:433
  39.3 1.8 %shard_map.103 = (f32[3,8,2,8,128]{4,3,2,1,0:T(8,128)}, f32[3,8,2,8,128]{4,3,2,1,0:T(8,128)}, f32[4,2,8,128]{3,2,1,0:T(8,128)}, f32[4,8,8]{2,1,0:T(8,128)}) custom-call(f32[3,8,2,8,128]{4,3,2,1,0:T(8,128)} %get-tuple-element.12.refs_0_, f32[3,8,2,8,128]{4,3,2,1,0:T(8,128)} %get-tuple-element.13.refs_1_, f32[4,2,8,128]{3,2,1,0:T(8,128)} %get-tuple-element.14.refs_2_, ...), custom_call_target="tpu_custom_call" | custom-call | tf_op jit(solution)/shard_map/pallas_call | solution.py:483

commit v5 on v4

--- a/solution.py
+++ b/solution.py
@@ -144,10 +144,12 @@
         zdst[0] = turned[0:8]
         zdst[1] = turned[Z - 8 : Z]
 
+    def x_sides(value, hx):
+        return (jnp.concatenate([hx[0][None], value[:-1]], axis=0),
+                jnp.concatenate([value[1:], hx[1][None]], axis=0))
+
     def neighbours(value, hx, hy, hz):
         shape = value.shape
-        x_lo = jnp.concatenate([hx[0][None], value[:-1]], axis=0)
-        x_hi = jnp.concatenate([value[1:], hx[1][None]], axis=0)
         y_lo = jnp.concatenate([hy[0][:, None], value[:, :-1]], axis=1)
         y_hi = jnp.concatenate([value[:, 1:], hy[1][:, None]], axis=1)
         flat = value.reshape(-1, Z)
@@ -156,7 +158,7 @@
             [hz[1], jnp.zeros((Z - 16, flat.shape[0]), jnp.float32), hz[0]], axis=0).T
         z_lo = pltpu.roll(jnp.where(lanes == Z - 1, turned, flat), 1, 1)
         z_hi = pltpu.roll(jnp.where(lanes == 0, turned, flat), Z - 1, 1)
-        return ((x_lo, x_hi), (y_lo, y_hi), (z_lo.reshape(shape), z_hi.reshape(shape)))
+        return (hx if hx is None else x_sides(value, hx), (y_lo, y_hi), (z_lo.reshape(shape), z_hi.reshape(shape)))
 
     def start_all(copies):
         for copy in copies:
@@ -229,8 +231,9 @@
     def publish(step, c, value):
         field_ref[step + 1, c] = value
         if step < STEPS:
+            send_all(plans[step][c][:4])
             z_faces(value, zs_ref.at[step, c])
-            send_all(plans[step][c])
+            send_all(plans[step][c][4:])
 
     for c in range(C):
         chunks[c].wait()
@@ -273,12 +276,15 @@
         drives.append(column)
 
     def advance(step, c):
-        recv_all(plans[step][c])
+        recv_all(plans[step][c][2:])
         current = field_ref[step + 1, c]
-        around = neighbours(current, hx_ref[step, c], hy_ref[step, c], hz_ref[step, c])
+        around = (None,) + neighbours(current, None, hy_ref[step, c], hz_ref[step, c])[1:]
         ramp = min(1.0, (step + 1) / ramp_steps)
         following = 2.0 * current - field_ref[step, c] + pushed * (ramp * drives[c])
-        for a in range(3):
+        for a in (1, 2, 0):
+            if a == 0:
+                recv_all(plans[step][c][:2])
+                around = (x_sides(current, hx_ref[step, c]),)
             for side in range(2):
                 following = following - coup_ref[0 if c == a else 1, a, side] * (current - around[a][side])
         publish(step + 1, c, following)

time: 41.3 us -> 40.7 us (0.985)
  Pallas kernels: 40.5 us -> 40 us
    pallas_call x1, Pallas kernels: 38.7 us -> 38.1 us  [shards(): pl.pallas_call(functools.partial(kernel, sizes), out_shape=shapes, in_spe...]
where the time goes in v5:
time: 40.7 us; the launch traced here: 40.6 us
  Pallas kernels  40 us (98%)
  between operations  0.64 us (2%)
    pallas_call x1, Pallas kernels, shards(): pl.pallas_call(functools.partial(kernel, sizes), out_shape=shapes, in_spe...  38.1 us
    pallas_call x1, Pallas kernels, shards(): pl.pallas_call(write_out, out_shape=shapes, in_specs=[hbm] * 4, out_specs...  1.84 us

profile of v5, /device:TPU:0, one launch (start us, length us, event | category | flops | bytes accessed | tf_op | source)
XLA Modules:
  0.0 40.6 jit_solution(5331677522225760493)
XLA Ops:
  0.6 38.1 %shard_map.102 = (f32[3,8,2,8,128]{4,3,2,1,0:T(8,128)}, f32[3,8,2,8,128]{4,3,2,1,0:T(8,128)}, f32[4,2,8,128]{3,2,1,0:T(8,128)}, f32[4,8,8]{2,1,0:T(8,128)}) custom-call(bf16[2,3,8,128,128]{4,3,2,1,0:T(8,128)(2,1)} %basis_hbm.1, bf16[8,128]{1,0:T(8,128)(2,1)} %bitcast.4, bf16[8,128]{1,0:T(8,128)(2,1)} %bitcast.5, s32[2,8,128]{2,1,0:T(8,128)} %ids_hbm.1, ...), custom_call_target="tpu_custom_call" | custom-call | flops 1000000000 | bytes 3000000 | tf_op jit(solution)/shard_map/pallas_call | solution.py:439
  38.8 1.8 %shard_map.103 = (f32[3,8,2,8,128]{4,3,2,1,0:T(8,128)}, f32[3,8,2,8,128]{4,3,2,1,0:T(8,128)}, f32[4,2,8,128]{3,2,1,0:T(8,128)}, f32[4,8,8]{2,1,0:T(8,128)}) custom-call(f32[3,8,2,8,128]{4,3,2,1,0:T(8,128)} %get-tuple-element.12.refs_0_, f32[3,8,2,8,128]{4,3,2,1,0:T(8,128)} %get-tuple-element.13.refs_1_, f32[4,2,8,128]{3,2,1,0:T(8,128)} %get-tuple-element.14.refs_2_, ...), custom_call_target="tpu_custom_call" | custom-call | tf_op jit(solution)/shard_map/pallas_call | solution.py:489

commit v6 on v5

--- a/solution.py
+++ b/solution.py
@@ -413,12 +413,15 @@
 def write_out(*refs):
     count = (len(refs) - 2) // 3
     sources, results, staged = (refs[count * i : count * (i + 1)] for i in range(3))
-    for ends, sem in ((zip(sources, staged), refs[-2]), (zip(staged, results), refs[-1])):
-        copies = [pltpu.make_async_copy(src, dst, sem.at[i]) for i, (src, dst) in enumerate(ends)]
-        for copy in copies:
-            copy.start()
-        for copy in copies:
-            copy.wait()
+    ins = [pltpu.make_async_copy(sources[i], staged[i], refs[-2].at[i]) for i in range(count)]
+    outs = [pltpu.make_async_copy(staged[i], results[i], refs[-1].at[i]) for i in range(count)]
+    for copy in ins:
+        copy.start()
+    for arrived, copy in zip(ins, outs):
+        arrived.wait()
+        copy.start()
+    for copy in outs:
+        copy.wait()
 
 
 def shards(sizes, basis, modal_now, modal_prev, material_ids, moduli, drive_mask, drive):

time: 40.7 us -> 40.7 us (level)
  no operation moved by 1% of the time
where the time goes in v6:
time: 40.7 us; the launch traced here: 40.5 us
  Pallas kernels  39.9 us (98%)
  between operations  0.64 us (2%)
    pallas_call x1, Pallas kernels, shards(): pl.pallas_call(functools.partial(kernel, sizes), out_shape=shapes, in_spe...  38.1 us
    pallas_call x1, Pallas kernels, shards(): pl.pallas_call(write_out, out_shape=shapes, in_specs=[hbm] * 4, out_specs...  1.77 us

profile of v6, /device:TPU:0, one launch (start us, length us, event | category | flops | bytes accessed | tf_op | source)
XLA Modules:
  0.0 40.5 jit_solution(8543411596970122072)
XLA Ops:
  0.6 38.1 %shard_map.102 = (f32[3,8,2,8,128]{4,3,2,1,0:T(8,128)}, f32[3,8,2,8,128]{4,3,2,1,0:T(8,128)}, f32[4,2,8,128]{3,2,1,0:T(8,128)}, f32[4,8,8]{2,1,0:T(8,128)}) custom-call(bf16[2,3,8,128,128]{4,3,2,1,0:T(8,128)(2,1)} %basis_hbm.1, bf16[8,128]{1,0:T(8,128)(2,1)} %bitcast.4, bf16[8,128]{1,0:T(8,128)(2,1)} %bitcast.5, s32[2,8,128]{2,1,0:T(8,128)} %ids_hbm.1, ...), custom_call_target="tpu_custom_call" | custom-call | flops 1000000000 | bytes 3000000 | tf_op jit(solution)/shard_map/pallas_call | solution.py:442
  38.8 1.8 %shard_map.103 = (f32[3,8,2,8,128]{4,3,2,1,0:T(8,128)}, f32[3,8,2,8,128]{4,3,2,1,0:T(8,128)}, f32[4,2,8,128]{3,2,1,0:T(8,128)}, f32[4,8,8]{2,1,0:T(8,128)}) custom-call(f32[3,8,2,8,128]{4,3,2,1,0:T(8,128)} %get-tuple-element.12.refs_0_, f32[3,8,2,8,128]{4,3,2,1,0:T(8,128)} %get-tuple-element.13.refs_1_, f32[4,2,8,128]{3,2,1,0:T(8,128)} %get-tuple-element.14.refs_2_, ...), custom_call_target="tpu_custom_call" | custom-call | tf_op jit(solution)/shard_map/pallas_call | solution.py:492
